TPU v7x, 128 devices: a whole 4x4x4 slice. The times are simulated.
128 devices in a mesh: ty: 8 (over x_lo, y), tx: 8 (over z, x_hi), slide: 2 (over core).
Axes of the slice: x: 4 (x_hi: 2, x_lo: 2; x = x_hi * 2 + x_lo), y: 4, z: 4, core: 2. Of those that a mesh axis runs over, the one named last changes fastest.
Arguments:
- tokens: bfloat16 [16, 8, 192, 768], P(('slide', 'ty'), 'tx'), parts along dimension 0, may hold values from -6 to 6
- summary: bfloat16 [2048, 768], P(('slide', 'ty', 'tx')), parts along dimension 0, may hold values from -6 to 6
- counts: int32 [16, 8], P('slide'), parts along dimension 0, may hold values from 1 to 192, as said below
- tile_pattern: int32 [16, 8, 9], P('slide'), parts along dimension 0, may hold values from 0 to 1, as said below
- summary_pattern: int32 [16, 8, 8], P(('slide', 'ty'), 'tx'), parts along dimension 0, may hold values 0 or 1
- norm_gain: float32 [768], replicated, may hold values from 0.1 to 1.9
- projections: bfloat16 [4, 768, 768], replicated, may hold values from -4 to 4
- cotangent: bfloat16 [16, 8, 192, 768], P(('slide', 'ty'), 'tx'), parts along dimension 0, may hold values from -6 to 6
Outputs:
- updated: bfloat16 [16, 8, 192, 768], P(('slide', 'ty'), 'tx'), parts along dimension 0
- grad_tokens: bfloat16 [16, 8, 192, 768], P(('slide', 'ty'), 'tx'), parts along dimension 0
- grad_summary: bfloat16 [2048, 768], P(('slide', 'ty', 'tx')), parts along dimension 0
- grad_proj: float32 [8, 768, 768], P('slide'), parts along dimension 0
- grad_gain: float32 [1536], P('slide'), parts along dimension 0
There are 2 independent parts, one for each index of `slide`. A program takes and returns all parts, laid end to end along the dimension named above; an argument that names none is the same for every part. Nothing has to cross between parts.
Inputs may be any that keep to these rules, and one draw needn't show every extreme that they name: `counts`: some tile holds exactly 192 tokens and some tile exactly 1 in every draw. `tile_pattern`: entry 4, the tile itself, is always 1.
All inputs are finite; a program needn't handle non-finite values. No bound on the sum of `summary_pattern` on one device may be relied on, other than what follows from the above.
Results may differ from a plain program's by a relative error of at most 0.011.
Values may be sent and summed in bfloat16 or wider, within the bound.
A program may use at most 128 MiB of HBM per device.

v0:
```python
import math

import jax
import jax.numpy as jnp
from jax import lax
from jax.sharding import Mesh
from jax.sharding import PartitionSpec as P

HEADS = 12
SBLK = 128
TY = ("ty_0", "ty_1")
TX = ("tx_0", "tx_1")
TY_TX = ("ty_0", "ty_1", "tx_0", "tx_1")
SLIDE_TY = ("slide", "ty_0", "ty_1")
SLIDE_TY_TX = ("slide", "ty_0", "ty_1", "tx_0", "tx_1")


epsilon = 1e-05


def sent_to_all(array, axis):
    peers = lax.axis_size(axis)
    return lax.all_to_all(
        jnp.broadcast_to(array[None], (peers, *array.shape)), axis, 0, 0, tiled=True
    )


def in_order(pieces, dim):
    lengths = list(pieces.shape[1:])
    lengths[dim] *= pieces.shape[0]
    return jnp.moveaxis(pieces, 0, dim).reshape(lengths)


def gathered_copies(array, axis, dim):
    pieces = sent_to_all(array, axis)
    return in_order(pieces, dim)


def with_halo(cells, sides, width):
    for axis, dim in sides:
        count = lax.axis_size(axis)
        ends = count - 1
        head = lax.slice_in_dim(cells, 0, width, axis=dim)
        tail = lax.slice_in_dim(cells, cells.shape[dim] - width, cells.shape[dim], axis=dim)
        cells = jnp.concatenate(
            [
                lax.ppermute(tail, axis, [(i, (i + 1) % count) for i in range(ends)]),
                cells,
                lax.ppermute(head, axis, [((i + 1) % count, i) for i in range(ends)]),
            ],
            axis=dim,
        )
    return cells


def passed_along(array, axis, by):
    peers = lax.axis_size(axis)
    pairs = [(i, i + by) for i in range(peers) if 0 <= i + by < peers]
    return lax.ppermute(array, axis, pairs)


def shortened(array):
    return jax.tree.map(lambda a: a.astype(jnp.bfloat16) if a.dtype == jnp.float32 else a, array)


def own_block(pieces, axes, turns):
    lengths = [lax.axis_size(a) for a in axes]
    pieces = pieces.reshape(*lengths, *pieces.shape[1:])
    pieces = pieces.transpose(*turns, *range(len(axes), pieces.ndim))
    pieces = pieces.reshape(-1, *pieces.shape[len(axes) :])
    for k in turns:
        pieces = lax.psum_scatter(pieces, axes[k], scatter_dimension=0, tiled=True)
    return pieces[0]


def cut_along(array, dim, peers):
    lengths = array.shape
    pieces = array.reshape(*lengths[:dim], peers, lengths[dim] // peers, *lengths[dim + 1 :])
    return jnp.moveaxis(pieces, dim, 0)


def summed_rows(array, axes, turns, dim):
    peers = lax.axis_size(axes)
    return own_block(cut_along(array, dim, peers), axes, turns)


def normalize(rows, gain):
    values = rows.astype(jnp.float32)
    scale = lax.rsqrt(jnp.mean(values * values, axis=-1, keepdims=True) + epsilon)
    return ((values * scale * gain).astype(jnp.bfloat16), scale)


def norm_back(rows, scale, gain, grad_norm):
    values = rows.astype(jnp.float32)
    scaled = gain * grad_norm
    return scale * scaled - values * scale**3 * jnp.mean(values * scaled, axis=-1, keepdims=True)


def project(rows, weight):
    return jnp.dot(rows, weight, preferred_element_type=jnp.float32).astype(jnp.bfloat16)


def back_project(rows, weight):
    return lax.dot_general(
        rows, weight, (((1,), (1,)), ((), ())), preferred_element_type=jnp.float32
    )


def exact_back(rows, weight):
    return lax.dot_general(
        rows, weight.astype(jnp.float32), (((1,), (1,)), ((), ())), precision=lax.Precision.HIGHEST
    )


def contract_rows(left, right):
    return lax.dot_general(
        left, right, (((0,), (0,)), ((), ())), preferred_element_type=jnp.float32
    )


def exact_rows(left, right):
    return lax.dot_general(
        left.astype(jnp.float32), right, (((0,), (0,)), ((), ())), precision=lax.Precision.HIGHEST
    )


def grouped(rows, group_width):
    return rows.reshape(rows.shape[0], -1, group_width).transpose(1, 0, 2)


def ungrouped(stacked):
    return stacked.transpose(1, 0, 2).reshape(stacked.shape[1], -1)


def head_scores(query_part, key_part, head_size, factor, allowed):
    query_heads = query_part.reshape(query_part.shape[0], -1, head_size)
    key_heads = key_part.reshape(key_part.shape[0], -1, head_size)
    scores = (
        jnp.einsum("qhd,khd->hqk", query_heads, key_heads, preferred_element_type=jnp.float32)
        * factor
    )
    return jnp.where(allowed[None, None, :], scores, -jnp.inf)


def softmax_grads(
    query_part, key_part, value_part, grad_part, log_totals, row_delta, allowed, head_size, factor
):
    scores = head_scores(query_part, key_part, head_size, factor, allowed)
    weights_full = jnp.exp(scores - log_totals[:, :, None])
    grad_heads = grad_part.reshape(grad_part.shape[0], -1, head_size)
    value_heads = value_part.reshape(value_part.shape[0], -1, head_size)
    grad_weights = jnp.einsum(
        "qhd,khd->hqk", grad_heads, value_heads, preferred_element_type=jnp.float32
    )
    row_delta = jnp.sum(weights_full * grad_weights, axis=-1)
    grad_scores = (weights_full * (grad_weights - row_delta[:, :, None])).astype(jnp.bfloat16)
    return (weights_full.astype(jnp.bfloat16), grad_scores, row_delta)


def key_side(grad_scores, weights_half, query_part, grad_part, head_size, factor):
    query_heads = query_part.reshape(query_part.shape[0], -1, head_size)
    grad_heads = grad_part.reshape(grad_part.shape[0], -1, head_size)
    key_grad = (
        jnp.einsum("hqk,qhd->khd", grad_scores, query_heads, preferred_element_type=jnp.float32)
        * factor
    )
    value_grad = jnp.einsum(
        "hqk,qhd->khd", weights_half, grad_heads, preferred_element_type=jnp.float32
    )
    return (key_grad.reshape(key_grad.shape[0], -1), value_grad.reshape(value_grad.shape[0], -1))


def local(
    tokens, summary, counts, tile_pattern, summary_pattern, norm_gain, projections, cotangent
):
    tile_rows = tokens.shape[2]
    model_width = tokens.shape[3]
    head_size = model_width // HEADS
    group_width = 2 * head_size
    factor = 1.0 / math.sqrt(head_size)
    near_rows = 9 * tile_rows
    zero = jnp.zeros((), jnp.int32)
    grid_row = lax.axis_index(TY)
    grid_col = lax.axis_index(TX)
    token_rows = tokens[0, 0]
    grads_in = cotangent[0, 0]
    w_query, w_key, w_value, w_out = (
        projections[0],
        projections[1],
        projections[2],
        projections[3],
    )
    hidden, row_scale = normalize(token_rows, norm_gain)
    summary_hidden, summary_scale = normalize(summary, norm_gain)
    queries = project(hidden, w_query)
    keys = project(hidden, w_key)
    values = project(hidden, w_value)
    piece = gathered_copies(summary_hidden, TY_TX, 0)
    every_summary = jnp.concatenate([project(piece, w_key), project(piece, w_value)], axis=1)
    own_pair = jnp.concatenate([keys, values], axis=1).reshape(1, 1, tile_rows, 2 * model_width)
    near_pairs = with_halo(own_pair, ((TY, 0), (TX, 1)), 1).reshape(near_rows, 2 * model_width)
    all_keys = jnp.concatenate(
        [near_pairs[:, :model_width], every_summary[:, :model_width]], axis=0
    )
    all_values = jnp.concatenate(
        [near_pairs[:, model_width:], every_summary[:, model_width:]], axis=0
    )
    count_pad = jnp.pad(counts, 1)
    near_counts = lax.dynamic_slice(count_pad, (grid_row, grid_col), (3, 3)).reshape(9)
    tile_flags = lax.dynamic_slice(tile_pattern, (grid_row, grid_col, zero), (1, 1, 9)).reshape(9)
    positions = jnp.arange(tile_rows, dtype=jnp.int32)
    tile_ok = ((positions[None, :] < near_counts[:, None]) & (tile_flags[:, None] == 1)).reshape(
        near_rows
    )
    summary_ok = jnp.repeat(summary_pattern[0, 0] == 1, SBLK)
    allowed = jnp.concatenate([tile_ok, summary_ok])
    own_valid = positions < near_counts[4]
    row_mask = own_valid.astype(jnp.float32)[:, None]
    query_groups = grouped(queries, group_width)
    key_groups = grouped(all_keys, group_width)
    value_groups = grouped(all_values, group_width)

    def forward_group(parts):
        query_part, key_part, value_part = parts
        scores = head_scores(query_part, key_part, head_size, factor, allowed)
        largest = jnp.max(scores, axis=-1, keepdims=True)
        exponent = jnp.exp(scores - largest)
        denominator = jnp.sum(exponent, axis=-1, keepdims=True)
        weights_half = (exponent / denominator).astype(jnp.bfloat16)
        value_heads = value_part.reshape(value_part.shape[0], -1, head_size)
        mixed = jnp.einsum(
            "hqk,khd->qhd", weights_half, value_heads, preferred_element_type=jnp.float32
        )
        return (
            mixed.reshape(mixed.shape[0], -1).astype(jnp.bfloat16),
            (largest + jnp.log(denominator))[:, :, 0],
        )

    attended_groups, log_totals = lax.map(forward_group, (query_groups, key_groups, value_groups))
    attended = ungrouped(attended_groups)
    mixed_rows = jnp.dot(attended, w_out, preferred_element_type=jnp.float32)
    updated = (token_rows.astype(jnp.float32) + row_mask * mixed_rows).astype(jnp.bfloat16)
    masked = grads_in * row_mask.astype(jnp.bfloat16)
    attended_grad = back_project(masked, w_out).astype(jnp.bfloat16)
    grad_groups = grouped(attended_grad, group_width)

    def query_group(parts):
        query_part, key_part, value_part, grad_part, log_part = parts
        weights_half, grad_scores, row_delta = softmax_grads(
            query_part, key_part, value_part, grad_part, log_part, None, allowed, head_size, factor
        )
        key_heads = key_part.reshape(key_part.shape[0], -1, head_size)
        query_grad = (
            jnp.einsum("hqk,khd->qhd", grad_scores, key_heads, preferred_element_type=jnp.float32)
            * factor
        )
        summ_kgrad, summ_vgrad = key_side(
            grad_scores[:, :, near_rows:],
            weights_half[:, :, near_rows:],
            query_part,
            grad_part,
            head_size,
            factor,
        )
        outputs = (query_grad.reshape(query_grad.shape[0], -1), summ_kgrad, summ_vgrad, row_delta)
        outputs = outputs + key_side(
            grad_scores[:, :, :near_rows],
            weights_half[:, :, :near_rows],
            query_part,
            grad_part,
            head_size,
            factor,
        )
        return outputs

    results = lax.map(
        query_group, (query_groups, key_groups, value_groups, grad_groups, log_totals)
    )
    query_grad = ungrouped(results[0]).astype(jnp.bfloat16)
    summary_part = jnp.concatenate([ungrouped(results[1]), ungrouped(results[2])], axis=1)
    row_delta = results[3]
    near_grad = jnp.concatenate([ungrouped(results[4]), ungrouped(results[5])], axis=1).reshape(
        3, 3, tile_rows, 2 * model_width
    )
    from_lower = passed_along(near_grad[:, 2].astype(jnp.bfloat16), TX, 1).astype(jnp.float32)
    from_upper = passed_along(near_grad[:, 0].astype(jnp.bfloat16), TX, -1).astype(jnp.float32)
    column_sum = near_grad[:, 1] + from_lower + from_upper
    row_lower = passed_along(shortened(column_sum[2]), TY, 1)
    row_upper = passed_along(shortened(column_sum[0]), TY, -1)
    own_grad = column_sum[1] + row_lower + row_upper
    key_grad = own_grad[:, :model_width].astype(jnp.bfloat16)
    value_grad = own_grad[:, model_width:].astype(jnp.bfloat16)
    summary_grad = summed_rows(summary_part, TY_TX, (1, 2, 0, 3), 0)
    summary_key_grad = summary_grad[:, :model_width]
    summary_value_grad = summary_grad[:, model_width:]
    summary_hidden_grad = exact_back(summary_key_grad, w_key) + exact_back(
        summary_value_grad, w_value
    )
    summary_key_proj = exact_rows(summary_hidden, summary_key_grad)
    summary_value_proj = exact_rows(summary_hidden, summary_value_grad)
    hidden_grad = (
        back_project(query_grad, w_query)
        + back_project(key_grad, w_key)
        + back_project(value_grad, w_value)
    )
    weight_part = jnp.stack(
        [
            contract_rows(hidden, query_grad),
            contract_rows(hidden, key_grad) + summary_key_proj,
            contract_rows(hidden, value_grad) + summary_value_proj,
            contract_rows(attended, masked),
        ]
    )
    gain_part = jnp.sum(hidden_grad * token_rows.astype(jnp.float32) * row_scale, axis=0) + jnp.sum(
        summary_hidden_grad * summary.astype(jnp.float32) * summary_scale, axis=0
    )
    grad_proj, grad_gain = lax.psum((weight_part, gain_part), TY_TX)
    grad_tokens = (
        grads_in.astype(jnp.float32) + norm_back(token_rows, row_scale, norm_gain, hidden_grad)
    ).astype(jnp.bfloat16)
    grad_summary = norm_back(summary, summary_scale, norm_gain, summary_hidden_grad).astype(
        jnp.bfloat16
    )
    return (
        updated.reshape(tokens.shape),
        grad_tokens.reshape(tokens.shape),
        grad_summary,
        grad_proj,
        grad_gain,
    )


def solution(mesh):
    finer = Mesh(
        mesh.devices.reshape(2, 4, 4, 2, mesh.shape["slide"]),
        ("ty_0", "ty_1", "tx_0", "tx_1", "slide"),
    )
    return jax.shard_map(
        local,
        mesh=finer,
        in_specs=(
            P(SLIDE_TY, TX, None, None),
            P(SLIDE_TY_TX, None),
            P("slide", None),
            P("slide", None, None),
            P(SLIDE_TY, TX, None),
            P(),
            P(),
            P(SLIDE_TY, TX, None, None),
        ),
        out_specs=(
            P(SLIDE_TY, TX, None, None),
            P(SLIDE_TY, TX, None, None),
            P(SLIDE_TY_TX, None),
            P("slide", None, None),
            P("slide"),
        ),
        check_vma=False,
    )
```

profile of v0, /device:TPU:0, one launch (start us, length us, event | category | flops | bytes accessed | tf_op | source)
XLA Modules:
  0.0 678.2 jit_solution(9434992536085312751)
XLA Ops:
  8.9 1.8 convolution_convert_fusion.4
  10.7 1.8 convolution_convert_fusion.5
  14.1 4.6 collective-permute-start
  21.9 13.6 %all-to-all-start = ((bf16[64,16,768]{2,1,0:T(8,128)(2,1)}), bf16[64,16,768]{2,1,0:T(8,128)(2,1)}, u32[]{:S(2)}, u32[]{:S(2)}) async-start(bf16[64,16,768]{2,1,0:T(8,128)(2,1)} %broadcast_in_dim.78), calls=%async_computation | async-start | bytes 3145728 | tf_op jit(solution)/shard_map/all_to_all | solution.py:23
  41.0 7.3 %collective-permute-start.2 = (bf16[3,1,192,1536]{3,2,1,0:T(8,128)(2,1)}, bf16[3,1,192,1536]{3,2,1,0:T(8,128)(2,1)}, u32[]{:S(2)}, u32[]{:S(2)}) collective-permute-start(bf16[3,1,192,1536]{3,2,1,0:T(8,128)(2,1)} %pad_maximum_fusion.4), channel_id=1, source_target_pairs={{0,2},{2,4},{4,6},{6,8},{8,10},{10,12},{12,14},{1,3},{3,5},{5,7},{... | collective-permute-start | bytes 5308424 | tf_op jit(solution)/shard_map/ppermute | solution.py:47
  50.4 1.8 convolution_convert_fusion.2
  53.8 6.3 all-to-all-done
  60.1 3.1 convolution_convert_fusion.1
  63.2 3.1 convolution_convert_fusion
  66.4 28.3 %collective-permute-done.3 = bf16[3,1,192,1536]{3,2,1,0:T(8,128)(2,1)} collective-permute-done((bf16[3,1,192,1536]{3,2,1,0:T(8,128)(2,1)}, bf16[3,1,192,1536]{3,2,1,0:T(8,128)(2,1)}, u32[]{:S(2)}, u32[]{:S(2)}) %collective-permute-start.3) | collective-permute-done | bytes 1769504 | tf_op jit(solution)/shard_map/ppermute | solution.py:49
  94.7 3.0 pad_maximum_fusion.1
  98.0 3.8 pad_maximum_fusion.2
  101.8 6.4 copy.21
  108.3 6.4 copy.22
  114.7 28.9 %while.30 = (s32[]{:T(128)}, bf16[6,192,128]{1,2,0:T(8,128)(2,1)}, f32[6,2,192]{2,1,0:T(2,128)S(1)}, bf16[6,2752,128]{1,2,0:T(8,128)(2,1)}, pred[2752]{0:T(1024)...) while((s32[]{:T(128)}, bf16[6,192,128]{1,2,0:T(8,128)(2,1)}, ...), condition=%wide.region_5.6_spmd, body=%wide.region_2.5_spmd.sunk | while | flops 279010944 | bytes 17236268 | solution.py:239
  143.6 69.4 %while.31 = (s32[]{:T(128)}, bf16[6,192,128]{1,2,0:T(8,128)(2,1)}, f32[6,1024,128]{1,2,0:T(8,128)}, f32[6,1024,128]{1,2,0:T(8,128)S(1)}, f32[6,1728,128]{1,2,0:T...) while((s32[]{:T(128)}, bf16[6,192,128]{1,2,0:T(8,128)(2,1)}, ...), condition=%wide.region_8.9_spmd, body=%wide.region_6.8_spmd.sunk | while | flops 686243456 | bytes 45984100 | solution.py:276
  213.0 3.4 copy.30
  216.4 3.2 concatenate.44
  219.6 4.9 copy.29
  224.5 4.9 concatenate.43
  229.4 2.7 maximum_bitcast_fusion
  232.1 3.1 copy.31
  235.3 7.8 %copy.26 = f32[1728,6,128]{2,1,0:T(8,128)} copy(f32[1728,6,128]{0,2,1:T(8,128)} %bitcast.285) | data formatting | bytes 10616832 | tf_op jit(solution)/shard_map/transpose | solution.py:132
  243.0 7.1 %concatenate.40 = f32[3,3,192,768]{3,2,1,0:T(8,128)} reshape(f32[1728,6,128]{2,1,0:T(8,128)} %copy.26) | data formatting | bytes 10616832 | tf_op jit(solution)/shard_map/concatenate | solution.py:282
  250.1 7.5 %copy.27 = f32[1728,6,128]{2,1,0:T(8,128)} copy(f32[1728,6,128]{0,2,1:T(8,128)} %bitcast.286) | data formatting | bytes 10616832 | tf_op jit(solution)/shard_map/transpose | solution.py:132
  257.6 7.1 %concatenate.41 = f32[3,3,192,768]{3,2,1,0:T(8,128)} reshape(f32[1728,6,128]{2,1,0:T(8,128)} %copy.27) | data formatting | bytes 10616832 | tf_op jit(solution)/shard_map/concatenate | solution.py:282
  264.7 3.4 constant_dynamic-update-slice_fusion.7
  269.5 4.1 copy-done
  273.6 3.1 convert.14
  276.6 58.0 %reduce-scatter.5.cloned.1.call-done = f32[16,16,1536]{2,1,0:T(8,128)} async-done(((f32[64,16,1536]{2,1,0:T(8,128)}), f32[16,16,1536]{2,1,0:T(8,128)}) %reduce-scatter.5.cloned.1.call-update) | async-done | bytes 1572880 | tf_op jit(solution)/shard_map/reduce_scatter | solution.py:72
  334.7 2.4 slice_bitcast_fusion.2
  338.5 6.3 collective-permute-start.4
  344.8 37.3 %collective-permute-done.5 = bf16[3,192,1536]{2,1,0:T(8,128)(2,1)S(1)} collective-permute-done((bf16[3,192,1536]{2,1,0:T(8,128)(2,1)S(1)}, bf16[3,192,1536]{2,1,0:T(8,128)(2,1)S(1)}, u32[]{:S(2)}, u32[]{:S(2)}) %collective-permute-start.5) | collective-permute-done | bytes 1769504 | tf_op jit(solution)/shard_map/ppermute | solution.py:59
  382.3 4.6 fusion.106
  389.4 5.4 collective-permute-start.6
  396.4 2.0 convolution_bitcast_fusion.1
  398.4 40.7 %reduce-scatter.9.cloned.1.call-done = f32[2,16,1536]{2,1,0:T(8,128)} async-done(((f32[4,16,1536]{2,1,0:T(8,128)}), f32[2,16,1536]{2,1,0:T(8,128)}) %reduce-scatter.9.cloned.1.call-update) | async-done | bytes 196624 | tf_op jit(solution)/shard_map/reduce_scatter | solution.py:72
  439.2 1.8 fusion.20
  441.0 19.7 %reduce-scatter.11.cloned.1.call-done = f32[1,16,1536]{2,1,0:T(8,128)} async-done(((f32[2,16,1536]{2,1,0:T(8,128)}), f32[1,16,1536]{2,1,0:T(8,128)}) %reduce-scatter.11.cloned.1.call-update) | async-done | bytes 98320 | tf_op jit(solution)/shard_map/reduce_scatter | solution.py:72
  460.7 1.9 fusion.94
  462.7 1.9 fusion.97
  466.9 4.0 pad_maximum_fusion
  471.9 2.6 fusion.36
  474.5 1.8 fusion.23
  476.4 1.9 convolution_add_fusion.1
  478.2 2.3 fusion.68
  483.8 179.1 %psum.15 = f32[768]{0:T(1024)} all-reduce(f32[768]{0:T(1024)S(1)} %add.134), channel_id=1, replica_groups=mesh['ty_0'=2,'ty_1'=4,'tx_0'=4,'tx_1'=2,'slide'=2] {'ty_0','ty_1','tx_0..., use_global_device_ids=true, to_apply=%region_18.19 | all-reduce | flops 768 | bytes 6144 | tf_op jit(solution)/shard_map/psum | solution.py:317
  663.6 8.0 %copy.71 = f32[4,768,768]{2,1,0:T(8,128)} copy(f32[4,768,768]{2,1,0:T(8,128)} %all-reduce.3.cloned.1.call-done) | data formatting | bytes 18874368
  (262 shorter events, 127.7 us)
Async XLA Ops:
  7.2 12.8 %copy-start.15 = (f32[768]{0:T(1024)S(1)}, f32[768]{0:T(1024)}, u32[]{:S(2)}) copy-start(f32[768]{0:T(1024)} %param.17) | copy-start | bytes 9220
  7.2 11.5 %copy-start.13 = (bf16[16,768]{1,0:T(8,128)(2,1)S(1)}, bf16[16,768]{1,0:T(8,128)(2,1)}, u32[]{:S(2)}) copy-start(bf16[16,768]{1,0:T(8,128)(2,1)} %param.13) | copy-start | bytes 73732
  8.9 26.9 %copy-start.17 = (f32[192]{0:T(256)}, f32[192]{0:T(256)S(1)}, u32[]{:S(2)}) copy-start(f32[192]{0:T(256)S(1)} %get-tuple-element.198) | copy-start | bytes 2308
  12.6 23.0 %copy-start.22 = (s32[8,8]{1,0:T(8,128)S(1)}, s32[8,8]{1,0:T(8,128)}, u32[]{:S(2)}) copy-start(s32[8,8]{1,0:T(8,128)} %param.14) | copy-start | bytes 772
  12.6 23.2 %copy-start.3 = (bf16[1,1,192,768]{3,2,1,0:T(8,128)(2,1)S(1)}, bf16[1,1,192,768]{3,2,1,0:T(8,128)(2,1)}, u32[]{:S(2)}) copy-start(bf16[1,1,192,768]{3,2,1,0:T(8,128)(2,1)} %param.12) | copy-start | bytes 884740
  12.6 25.6 %collective-permute-start.1 = (bf16[1,1,192,1536]{3,2,1,0:T(8,128)(2,1)S(1)}, bf16[1,1,192,1536]{3,2,1,0:T(8,128)(2,1)S(1)}, u32[]{:S(2)}, u32[]{:S(2)}) collective-permute-start(bf16[1,1,192,1536]{3,2,1,0:T(8,128)(2,1)S(1)} %maximum_bitcast_fusion.1), channel_id=1, source_target_pairs={{16,0},{32,16},{48,32},{64,48},{80,64},{96,80},{112,96},{17,1},{33... | collective-permute-start | bytes 1769480 | tf_op jit(solution)/shard_map/ppermute | solution.py:49
  14.1 24.2 %collective-permute-start = (bf16[1,1,192,1536]{3,2,1,0:T(8,128)(2,1)S(1)}, bf16[1,1,192,1536]{3,2,1,0:T(8,128)(2,1)S(1)}, u32[]{:S(2)}, u32[]{:S(2)}) collective-permute-start(bf16[1,1,192,1536]{3,2,1,0:T(8,128)(2,1)S(1)} %maximum_bitcast_fusion.1), channel_id=1, source_target_pairs={{0,16},{16,32},{32,48},{48,64},{64,80},{80,96},{96,112},{1,17},{17... | collective-permute-start | bytes 1769480 | tf_op jit(solution)/shard_map/ppermute | solution.py:47
  19.4 0.6 copy-start.19
  20.1 0.6 copy-start.10
  21.9 38.2 %all-to-all-start = ((bf16[64,16,768]{2,1,0:T(8,128)(2,1)}), bf16[64,16,768]{2,1,0:T(8,128)(2,1)}, u32[]{:S(2)}, u32[]{:S(2)}) async-start(bf16[64,16,768]{2,1,0:T(8,128)(2,1)} %broadcast_in_dim.78), calls=%async_computation | async-start | bytes 3145728 | tf_op jit(solution)/shard_map/all_to_all | solution.py:23
  35.5 299.1 %reduce-scatter.5.cloned.1.call-start = ((), (), s32[]{:S(2)}) async-start(), calls=%async_computation.5 | async-start | bytes 7864320 | tf_op jit(solution)/shard_map/reduce_scatter | solution.py:72
  35.8 14.6 %copy-start.8 = (bf16[1,1,192,768]{3,2,1,0:T(8,128)(2,1)S(1)}, bf16[1,1,192,768]{3,2,1,0:T(8,128)(2,1)}, u32[]{:S(2)}) copy-start(bf16[1,1,192,768]{3,2,1,0:T(8,128)(2,1)} %param.19) | copy-start | bytes 884740
  38.3 15.3 %copy-start.26 = (s32[1,1,8]{2,1,0:T(1,128)S(1)}, s32[1,1,8]{2,1,0:T(1,128)}, u32[]{:S(2)}) copy-start(s32[1,1,8]{2,1,0:T(1,128)} %param.16) | copy-start | bytes 100
  39.7 55.0 %collective-permute-start.3 = (bf16[3,1,192,1536]{3,2,1,0:T(8,128)(2,1)}, bf16[3,1,192,1536]{3,2,1,0:T(8,128)(2,1)}, u32[]{:S(2)}, u32[]{:S(2)}) collective-permute-start(bf16[3,1,192,1536]{3,2,1,0:T(8,128)(2,1)} %pad_maximum_fusion.4), channel_id=1, source_target_pairs={{2,0},{4,2},{6,4},{8,6},{10,8},{12,10},{14,12},{3,1},{5,3},{7,5},{... | collective-permute-start | bytes 5308424 | tf_op jit(solution)/shard_map/ppermute | solution.py:49
  41.0 53.7 %collective-permute-start.2 = (bf16[3,1,192,1536]{3,2,1,0:T(8,128)(2,1)}, bf16[3,1,192,1536]{3,2,1,0:T(8,128)(2,1)}, u32[]{:S(2)}, u32[]{:S(2)}) collective-permute-start(bf16[3,1,192,1536]{3,2,1,0:T(8,128)(2,1)} %pad_maximum_fusion.4), channel_id=1, source_target_pairs={{0,2},{2,4},{4,6},{6,8},{8,10},{10,12},{12,14},{1,3},{3,5},{5,7},{... | collective-permute-start | bytes 5308424 | tf_op jit(solution)/shard_map/ppermute | solution.py:47
  50.4 3.2 copy-start.24
  114.7 28.9 %copy-start.5 = (f32[6,1024,128]{1,2,0:T(8,128)S(1)}, f32[6,1024,128]{1,2,0:T(8,128)}, u32[]{:S(2)}) copy-start(f32[6,1024,128]{1,2,0:T(8,128)} %custom-call.5) | copy-start | bytes 9437188
  235.2 151.7 %reduce-scatter.7.cloned.1.call-start = ((), (), s32[]{:S(2)}) async-start(), calls=%async_computation.6 | async-start | bytes 1966080 | tf_op jit(solution)/shard_map/reduce_scatter | solution.py:72
  264.7 4.1 copy-start.1
  269.5 4.1 copy-start
  334.7 104.4 %reduce-scatter.9.cloned.1.call-start = ((), (), s32[]{:S(2)}) async-start(), calls=%async_computation.7 | async-start | bytes 589824 | tf_op jit(solution)/shard_map/reduce_scatter | solution.py:72
  337.1 44.9 %collective-permute-start.5 = (bf16[3,192,1536]{2,1,0:T(8,128)(2,1)S(1)}, bf16[3,192,1536]{2,1,0:T(8,128)(2,1)S(1)}, u32[]{:S(2)}, u32[]{:S(2)}) collective-permute-start(bf16[3,192,1536]{2,1,0:T(8,128)(2,1)S(1)} %get-tuple-element.192), channel_id=1, source_target_pairs={{2,0},{4,2},{6,4},{8,6},{10,8},{12,10},{14,12},{3,1},{5,3},{7,5},{... | collective-permute-start | bytes 5308424 | tf_op jit(solution)/shard_map/ppermute | solution.py:59
  338.4 56.4 %copy-start.9 = (bf16[1,1,192,768]{3,2,1,0:T(8,128)(2,1)S(1)}, bf16[1,1,192,768]{3,2,1,0:T(8,128)(2,1)}, u32[]{:S(2)}) copy-start(bf16[1,1,192,768]{3,2,1,0:T(8,128)(2,1)} %param.19) | copy-start | bytes 884740
  338.5 56.3 %copy-start.25 = (bf16[192]{0:T(256)(128)(2,1)S(1)}, bf16[192]{0:T(256)(128)(2,1)}, u32[]{:S(2)}) copy-start(bf16[192]{0:T(256)(128)(2,1)} %copy-done.24) | copy-start | bytes 1156
  338.5 43.8 %collective-permute-start.4 = (bf16[3,192,1536]{2,1,0:T(8,128)(2,1)S(1)}, bf16[3,192,1536]{2,1,0:T(8,128)(2,1)S(1)}, u32[]{:S(2)}, u32[]{:S(2)}) collective-permute-start(bf16[3,192,1536]{2,1,0:T(8,128)(2,1)S(1)} %get-tuple-element.191), channel_id=1, source_target_pairs={{0,2},{2,4},{4,6},{6,8},{8,10},{10,12},{12,14},{1,3},{3,5},{5,7},{... | collective-permute-start | bytes 5308424 | tf_op jit(solution)/shard_map/ppermute | solution.py:59
  386.9 9.4 %copy-start.4 = (bf16[1,1,192,768]{3,2,1,0:T(8,128)(2,1)S(1)}, bf16[1,1,192,768]{3,2,1,0:T(8,128)(2,1)}, u32[]{:S(2)}) copy-start(bf16[1,1,192,768]{3,2,1,0:T(8,128)(2,1)} %param.12) | copy-start | bytes 884740
  386.9 9.4 %copy-start.6 = (bf16[6,192,128]{1,2,0:T(8,128)(2,1)S(1)}, bf16[6,192,128]{1,2,0:T(8,128)(2,1)}, u32[]{:S(2)}) copy-start(bf16[6,192,128]{1,2,0:T(8,128)(2,1)} %get-tuple-element.111) | copy-start | bytes 884740
  386.9 9.4 %copy-start.16 = (f32[768]{0:T(1024)S(1)}, f32[768]{0:T(1024)}, u32[]{:S(2)}) copy-start(f32[768]{0:T(1024)} %param.17) | copy-start | bytes 9220
  386.9 9.4 %copy-start.18 = (f32[192]{0:T(256)S(1)}, f32[192]{0:T(256)}, u32[]{:S(2)}) copy-start(f32[192]{0:T(256)} %copy-done.17) | copy-start | bytes 2308
  387.0 73.7 %reduce-scatter.11.cloned.1.call-start = ((), (), s32[]{:S(2)}) async-start(), calls=%async_computation.8 | async-start | bytes 294912 | tf_op jit(solution)/shard_map/reduce_scatter | solution.py:72
  388.1 51.1 %collective-permute-start.7 = (bf16[192,1536]{1,0:T(8,128)(2,1)}, bf16[192,1536]{1,0:T(8,128)(2,1)}, u32[]{:S(2)}, u32[]{:S(2)}) collective-permute-start(bf16[192,1536]{1,0:T(8,128)(2,1)} %get-tuple-element.196), channel_id=1, source_target_pairs={{16,0},{32,16},{48,32},{64,48},{80,64},{96,80},{112,96},{17,1},{33... | collective-permute-start | bytes 1769480 | tf_op jit(solution)/shard_map/ppermute | solution.py:59
  389.4 49.8 %collective-permute-start.6 = (bf16[192,1536]{1,0:T(8,128)(2,1)}, bf16[192,1536]{1,0:T(8,128)(2,1)}, u32[]{:S(2)}, u32[]{:S(2)}) collective-permute-start(bf16[192,1536]{1,0:T(8,128)(2,1)} %get-tuple-element.195), channel_id=1, source_target_pairs={{0,16},{16,32},{32,48},{48,64},{64,80},{80,96},{96,112},{1,17},{17... | collective-permute-start | bytes 1769480 | tf_op jit(solution)/shard_map/ppermute | solution.py:59
  439.1 224.5 %all-reduce.3.cloned.1.call-start = ((), (), s32[]{:S(2)}) async-start(), calls=%async_computation.9 | async-start | bytes 18874368 | tf_op jit(solution)/shard_map/psum | solution.py:317
  465.2 1.7 copy-start.2
  470.9 1.0 copy-start.11
  470.9 3.6 copy-start.7
  470.9 10.6 %slice-start = ((s8[4718592]{0:T(1024)(128)(4,1)}), s8[524288]{0:T(1024)(128)(4,1)S(1)}, s32[]{:S(2)}) async-start(s8[4718592]{0:T(1024)(128)(4,1)} %bitcast.287), calls=%async_computation.10 | async-start | bytes 1048576
  471.9 9.6 %slice-start.1 = ((s8[4718592]{0:T(1024)(128)(4,1)}), s8[4194304]{0:T(1024)(128)(4,1)S(1)}, s32[]{:S(2)}) async-start(s8[4718592]{0:T(1024)(128)(4,1)} %bitcast.287), calls=%async_computation.11 | async-start | bytes 8388608
  474.5 6.1 copy-start.21
  476.3 5.2 copy-start.12
  478.2 4.4 copy-start.14
  478.2 4.4 copy-start.20
  478.2 184.7 %copy-start.23 = (f32[16]{0:T(128)S(1)}, f32[16]{0:T(128)}, u32[]{:S(2)}) copy-start(f32[16]{0:T(128)} %get-tuple-element.199) | copy-start | bytes 196
Sparse Core Ops, SparseCore 0:
  235.3 99.2 reduce-scatter.4
  337.1 25.5 reduce-scatter.6
  387.1 51.9 reduce-scatter.8
  441.4 19.2 reduce-scatter.10
  471.1 174.1 all-reduce.2
where the time goes:
time: 681 us; the launch traced here: 678 us
  waiting for transfers between devices  191 us (28%)
  blocking collectives  179 us (26%)
  local copies, waits for them, and re-layouts  139 us (20%)
  matrix products  72.4 us (11%)
  starting transfers between devices  42.7 us (6%)
  other arithmetic  39.7 us (6%)
  between operations  14.3 us (2%)
    psum x1, blocking collectives, local(): grad_proj, grad_gain = lax.psum((weight_part, gain_part), TY_TX)  179 us
    reduce_scatter x4, waiting for transfers between devices, own_block(): pieces = lax.psum_scatter(pieces, axes[k], scatter_dimension=0, tiled=True)  118 us
    ppermute x4, waiting for transfers between devices, passed_along(): return lax.ppermute(array, axis, pairs)  37.5 us
    ppermute x2, waiting for transfers between devices, with_halo(): lax.ppermute(head, axis, [((i + 1) % count, i) for i in range(ends)])  28.3 us
    dynamic_slice x36, local copies, waits for them, and re-layouts, local(): lax.map(forward_group, (query_groups, key_groups, value_groups))  27.8 us
    transpose x4, local copies, waits for them, and re-layouts, ungrouped(): return stacked.transpose(1, 0, 2).reshape(stacked.shape[1], -1)  23.6 us
    unnamed x60, local copies, waits for them, and re-layouts  18.7 us
    dynamic_update_slice x18, local copies, waits for them, and re-layouts, local(): lax.map(query_group, (query_groups, key_groups, value_groups, grad_groups...  17.7 us
  transfers between devices with their start and end apart: 14, of which 7 were waited for; matrix products, arithmetic and copies ran while one was open for 12% of the time, Pallas kernels for 0%

commit v1 on v0

v1 whole, which is shorter than its diff:
```python
import math

import jax
import jax.numpy as jnp
from jax import lax
from jax.experimental import pallas as pl
from jax.experimental.pallas import tpu as pltpu
from jax.sharding import Mesh
from jax.sharding import PartitionSpec as P

HEADS = 12
SBLK = 128
QUAD = 4
CHUNK = 256
PACK = 16
NEAR = 9
TY = ("ty_0", "ty_1")
TX = ("tx_0", "tx_1")
TY_TX = ("ty_0", "ty_1", "tx_0", "tx_1")
SLIDE_TY = ("slide", "ty_0", "ty_1")
SLIDE_TY_TX = ("slide", "ty_0", "ty_1", "tx_0", "tx_1")
F32 = jnp.float32
BF16 = jnp.bfloat16

epsilon = 1e-05


def with_halo(cells, sides, width):
    for axis, dim in sides:
        count = lax.axis_size(axis)
        ends = count - 1
        head = lax.slice_in_dim(cells, 0, width, axis=dim)
        tail = lax.slice_in_dim(cells, cells.shape[dim] - width, cells.shape[dim], axis=dim)
        cells = jnp.concatenate(
            [
                lax.ppermute(tail, axis, [(i, (i + 1) % count) for i in range(ends)]),
                cells,
                lax.ppermute(head, axis, [((i + 1) % count, i) for i in range(ends)]),
            ],
            axis=dim,
        )
    return cells


def passed_along(array, axis, by):
    peers = lax.axis_size(axis)
    pairs = [(i, i + by) for i in range(peers) if 0 <= i + by < peers]
    return lax.ppermute(array, axis, pairs)


def own_block(pieces, axes, turns):
    lengths = [lax.axis_size(a) for a in axes]
    pieces = pieces.reshape(*lengths, *pieces.shape[1:])
    pieces = pieces.transpose(*turns, *range(len(axes), pieces.ndim))
    pieces = pieces.reshape(-1, *pieces.shape[len(axes) :])
    for k in turns:
        pieces = lax.psum_scatter(pieces, axes[k], scatter_dimension=0, tiled=True)
    return pieces[0]


def normalize(rows, gain):
    values = rows.astype(F32)
    scale = lax.rsqrt(jnp.mean(values * values, axis=-1, keepdims=True) + epsilon)
    return ((values * scale * gain).astype(BF16), scale)


def norm_back(rows, scale, gain, grad_norm):
    values = rows.astype(F32)
    scaled = gain * grad_norm
    return scale * scaled - values * scale**3 * jnp.mean(values * scaled, axis=-1, keepdims=True)


def dot(a, b, ca, cb):
    return lax.dot_general(a, b, (((ca,), (cb,)), ((), ())), preferred_element_type=F32)


def layer_kernel(
    meta, near, summ, w, tok, cot,
    updated, near_grad, own_grad, sum_grad, w_part, gain_part,
    xp, kp, vp, dkt, dvt, scores, probs, bias, qs, gs, qst, gst, acc, m_ref, l_ref, d_ref,
    q_all, g_all, o_all, dq_all,
):
    rows = tok.shape[0]
    width = tok.shape[1]
    quads = width // CHUNK
    head_size = width // HEADS
    stack = QUAD * rows
    factor = 1.0 / math.sqrt(head_size)
    n_blocks = summ.shape[0] // SBLK
    yp = kp
    zk = scores.at[:, 0:width]
    zv = scores.at[:, width : 2 * width]

    block_at = []
    total = jnp.int32(0)
    for b in range(n_blocks):
        block_at.append(total)
        flag = meta[NEAR + b]

        @pl.when(flag == 1)
        def _(b=b, total=total):
            xp[pl.ds(pl.multiple_of(total, SBLK), SBLK), :] = summ[b * SBLK : (b + 1) * SBLK, :]

        total = total + SBLK * flag
    summ_end = total
    tile_at = []
    for t in range(NEAR):
        tile_at.append(total)
        n = meta[t]

        @pl.when(n > 0)
        def _(t=t, total=total):
            xp[pl.ds(pl.multiple_of(total, PACK), rows), :] = near[t]

        total = total + ((n + (PACK - 1)) // PACK) * PACK
    xp[pl.ds(pl.multiple_of(total, PACK), CHUNK), :] = jnp.zeros((CHUNK, width), BF16)
    chunks = (total + (CHUNK - 1)) // CHUNK

    place = lax.broadcasted_iota(jnp.int32, bias.shape, 1)
    live = place < summ_end
    for t in range(NEAR):
        live = live | ((place >= tile_at[t]) & (place < tile_at[t] + meta[t]))
    bias[...] = jnp.where(live, 0.0, -1e30)

    own = near[NEAR // 2]
    valid = lax.broadcasted_iota(jnp.int32, (rows, width), 0) < meta[NEAR + n_blocks]
    masked = jnp.where(valid, cot[...].astype(F32), 0.0).astype(BF16)
    q_all[...] = (dot(own, w[0], 1, 0).astype(BF16).astype(F32) * factor).astype(BF16)
    g_all[...] = dot(masked, w[3], 1, 1).astype(BF16)

    def project(c, carry):
        at = pl.ds(pl.multiple_of(c * CHUNK, CHUNK), CHUNK)
        x = xp[at, :]
        kp[at, :] = dot(x, w[1], 1, 0).astype(BF16)
        vp[at, :] = dot(x, w[2], 1, 0).astype(BF16)
        return carry

    lax.fori_loop(0, chunks, project, 0)

    lane_head = lax.broadcasted_iota(jnp.int32, (rows, CHUNK), 1) // head_size
    low, high = slice(0, 128), slice(128, 256)

    for j in range(quads):
        cols = slice(j * CHUNK, (j + 1) * CHUNK)
        q_part = q_all[:, cols].astype(F32)
        g_part = g_all[:, cols].astype(F32)
        for i in range(QUAD):
            here = slice(i * rows, (i + 1) * rows)
            qs[here, :] = jnp.where(lane_head == i, q_part, 0.0).astype(BF16)
            gs[here, :] = jnp.where(lane_head == i, g_part, 0.0).astype(BF16)
        m_ref[...] = jnp.full(m_ref.shape, -3e38, F32)

        def score(c, carry):
            at = pl.ds(pl.multiple_of(c * CHUNK, CHUNK), CHUNK)
            s = dot(qs[...], kp[at, cols], 1, 1) + bias[0:1, at]
            scores[:, at] = s
            m_ref[...] = jnp.maximum(m_ref[...], jnp.maximum(s[:, low], s[:, high]))
            return carry

        lax.fori_loop(0, chunks, score, 0)
        m_ref[...] = jnp.broadcast_to(jnp.max(m_ref[...], axis=1, keepdims=True), m_ref.shape)
        l_ref[...] = jnp.zeros(l_ref.shape, F32)
        acc[...] = jnp.zeros(acc.shape, F32)

        def mix(c, carry):
            at = pl.ds(pl.multiple_of(c * CHUNK, CHUNK), CHUNK)
            s = scores[:, at]
            m = m_ref[...]
            e0 = jnp.exp(s[:, low] - m)
            e1 = jnp.exp(s[:, high] - m)
            l_ref[...] += e0 + e1
            e = jnp.concatenate([e0, e1], axis=1).astype(BF16)
            probs[:, at] = e
            acc[...] += dot(e, vp[at, cols], 1, 0)
            return carry

        lax.fori_loop(0, chunks, mix, 0)
        inv = 1.0 / jnp.sum(l_ref[...], axis=1, keepdims=True)
        out = acc[...] * inv
        d_ref[...] = jnp.broadcast_to(
            jnp.sum(out * gs[...].astype(F32), axis=1, keepdims=True), d_ref.shape
        )
        picked = jnp.zeros((rows, CHUNK), F32)
        for i in range(QUAD):
            here = slice(i * rows, (i + 1) * rows)
            picked = jnp.where(lane_head == i, out[here], picked)
        o_all[:, cols] = picked.astype(BF16)
        qst[...] = (qs[...].astype(F32) * inv).astype(BF16).T
        gst[...] = (gs[...].astype(F32) * inv).astype(BF16).T
        l_ref[...] = jnp.broadcast_to(inv, l_ref.shape)
        acc[...] = jnp.zeros(acc.shape, F32)

        def back(c, carry):
            at = pl.ds(pl.multiple_of(c * CHUNK, CHUNK), CHUNK)
            e = probs[:, at]
            dp = dot(gs[...], vp[at, cols], 1, 1)
            d = d_ref[...]
            delta = jnp.concatenate([dp[:, low] - d, dp[:, high] - d], axis=1)
            ds = (e.astype(F32) * delta).astype(BF16)
            acc[...] += dot(ds, kp[at, cols], 1, 0)
            dkt[cols, at] = dot(qst[...], ds, 1, 0).astype(BF16)
            dvt[cols, at] = dot(gst[...], e, 1, 0).astype(BF16)
            return carry

        lax.fori_loop(0, chunks, back, 0)
        inv2 = l_ref[...] * factor
        dq = acc[...] * jnp.concatenate([inv2, inv2], axis=1)
        picked = jnp.zeros((rows, CHUNK), F32)
        for i in range(QUAD):
            here = slice(i * rows, (i + 1) * rows)
            picked = jnp.where(lane_head == i, dq[here], picked)
        dq_all[:, cols] = picked.astype(BF16)

    zk[...] = jnp.zeros(zk.shape, F32)
    zv[...] = jnp.zeros(zv.shape, F32)
    own_part = dot(dq_all[...], w[0], 1, 1)
    gain_part[...] = jnp.sum(
        (own_part * own.astype(F32)).reshape(rows // 8, 8, width), axis=0
    )

    def finish(c, carry):
        at = pl.ds(pl.multiple_of(c * CHUNK, CHUNK), CHUNK)
        x = xp[at, :]
        dk = dkt[:, at]
        dv = dvt[:, at]
        zk[...] += dot(dk, x, 1, 0)
        zv[...] += dot(dv, x, 1, 0)
        yt = dot(w[1], dk, 1, 0) + dot(w[2], dv, 1, 0)
        y = yt.astype(BF16).T
        yp[at, :] = y
        gain_part[...] += jnp.sum(
            (y.astype(F32) * x.astype(F32)).reshape(CHUNK // 8, 8, width), axis=0
        )
        return carry

    lax.fori_loop(0, chunks, finish, 0)

    w_part[0] = dot(own, dq_all[...], 0, 0).astype(BF16)
    w_part[1] = zk[...].astype(BF16).T
    w_part[2] = zv[...].astype(BF16).T
    w_part[3] = dot(o_all[...], masked, 0, 0).astype(BF16)

    row_at = lax.broadcasted_iota(jnp.int32, (rows, width), 0)
    for t in range(NEAR):
        y = yp[pl.ds(pl.multiple_of(tile_at[t], PACK), rows), :].astype(F32)
        y = jnp.where(row_at < meta[t], y, 0.0)
        if t == NEAR // 2:
            own_grad[...] = y + own_part
            near_grad[t] = jnp.zeros((rows, width), BF16)
        else:
            near_grad[t] = y.astype(BF16)
    for b in range(n_blocks):
        y = yp[pl.ds(pl.multiple_of(block_at[b], SBLK), SBLK), :].astype(F32)
        keep = jnp.zeros((SBLK, width), jnp.int32) + meta[NEAR + b]
        sum_grad[b * SBLK : (b + 1) * SBLK, :] = jnp.where(keep == 1, y, 0.0).astype(BF16)

    mixed = dot(o_all[...], w[3], 1, 0)
    updated[...] = (tok[...].astype(F32) + jnp.where(valid, mixed, 0.0)).astype(BF16)


def layer(meta, near, summ, w, tok, cot):
    rows, width = tok.shape
    most = (NEAR * rows + summ.shape[0] + CHUNK - 1) // CHUNK * CHUNK
    stack = QUAD * rows
    vm = pl.BlockSpec(memory_space=pltpu.VMEM)
    return pl.pallas_call(
        layer_kernel,
        out_shape=(
            jax.ShapeDtypeStruct((rows, width), BF16),
            jax.ShapeDtypeStruct((NEAR, rows, width), BF16),
            jax.ShapeDtypeStruct((rows, width), F32),
            jax.ShapeDtypeStruct(summ.shape, BF16),
            jax.ShapeDtypeStruct((4, width, width), BF16),
            jax.ShapeDtypeStruct((8, width), F32),
        ),
        in_specs=[pl.BlockSpec(memory_space=pltpu.SMEM)] + [vm] * 5,
        out_specs=(vm,) * 6,
        scratch_shapes=[
            pltpu.VMEM((most + CHUNK, width), BF16),
            pltpu.VMEM((most + CHUNK, width), BF16),
            pltpu.VMEM((most, width), BF16),
            pltpu.VMEM((width, most), BF16),
            pltpu.VMEM((width, most), BF16),
            pltpu.VMEM((stack, most), F32),
            pltpu.VMEM((stack, most), BF16),
            pltpu.VMEM((8, most), F32),
            pltpu.VMEM((stack, CHUNK), BF16),
            pltpu.VMEM((stack, CHUNK), BF16),
            pltpu.VMEM((CHUNK, stack), BF16),
            pltpu.VMEM((CHUNK, stack), BF16),
            pltpu.VMEM((stack, CHUNK), F32),
            pltpu.VMEM((stack, 128), F32),
            pltpu.VMEM((stack, 128), F32),
            pltpu.VMEM((stack, 128), F32),
            pltpu.VMEM((rows, width), BF16),
            pltpu.VMEM((rows, width), BF16),
            pltpu.VMEM((rows, width), BF16),
            pltpu.VMEM((rows, width), BF16),
        ],
        compiler_params=pltpu.CompilerParams(vmem_limit_bytes=63 * 1024 * 1024),
        name="layer",
    )(meta, near, summ, w, tok, cot)


def local(
    tokens, summary, counts, tile_pattern, summary_pattern, norm_gain, projections, cotangent
):
    rows, width = tokens.shape[2:]
    zero = jnp.zeros((), jnp.int32)
    grid_row = lax.axis_index(TY)
    grid_col = lax.axis_index(TX)
    token_rows = tokens[0, 0]
    grads_in = cotangent[0, 0]
    hidden, row_scale = normalize(token_rows, norm_gain)
    summary_hidden, summary_scale = normalize(summary, norm_gain)
    every = lax.all_gather(summary_hidden, TY_TX, axis=0, tiled=True)
    near = with_halo(hidden.reshape(1, 1, rows, width), ((TX, 1), (TY, 0)), 1)
    near = near.reshape(NEAR, rows, width)
    count_pad = jnp.pad(counts, 1)
    near_counts = lax.dynamic_slice(count_pad, (grid_row, grid_col), (3, 3)).reshape(NEAR)
    flags = lax.dynamic_slice(tile_pattern, (grid_row, grid_col, zero), (1, 1, NEAR)).reshape(NEAR)
    meta = jnp.concatenate(
        [
            jnp.where(flags == 1, near_counts, 0),
            (summary_pattern[0, 0] == 1).astype(jnp.int32),
            near_counts[NEAR // 2 : NEAR // 2 + 1],
        ]
    )
    updated, near_grad, own_grad, sum_grad, w_part, gain_part = layer(
        meta, near, every, projections, token_rows, grads_in
    )
    near_grad = near_grad.reshape(3, 3, rows, width)
    row_lower = passed_along(near_grad[2], TY, 1).astype(F32)
    row_upper = passed_along(near_grad[0], TY, -1).astype(F32)
    row_sum = near_grad[1].astype(F32) + row_lower + row_upper
    from_lower = passed_along(row_sum[2].astype(BF16), TX, 1).astype(F32)
    from_upper = passed_along(row_sum[0].astype(BF16), TX, -1).astype(F32)
    hidden_grad = own_grad + row_sum[1] + from_lower + from_upper
    pieces = sum_grad.reshape(-1, summary.shape[0], width)
    summary_hidden_grad = own_block(pieces, TY_TX, (1, 2, 0, 3)).astype(F32)
    grad_proj = lax.psum(w_part, TY_TX).astype(F32)
    grad_gain = lax.psum(jnp.sum(gain_part, axis=0), TY_TX)
    grad_gain = grad_gain / norm_gain
    grad_tokens = (
        grads_in.astype(F32) + norm_back(token_rows, row_scale, norm_gain, hidden_grad)
    ).astype(BF16)
    grad_summary = norm_back(summary, summary_scale, norm_gain, summary_hidden_grad).astype(BF16)
    return (
        updated.reshape(tokens.shape),
        grad_tokens.reshape(tokens.shape),
        grad_summary,
        grad_proj,
        grad_gain,
    )


def solution(mesh):
    finer = Mesh(
        mesh.devices.reshape(2, 4, 4, 2, mesh.shape["slide"]),
        ("ty_0", "ty_1", "tx_0", "tx_1", "slide"),
    )
    return jax.shard_map(
        local,
        mesh=finer,
        in_specs=(
            P(SLIDE_TY, TX, None, None),
            P(SLIDE_TY_TX, None),
            P("slide", None),
            P("slide", None, None),
            P(SLIDE_TY, TX, None),
            P(),
            P(),
            P(SLIDE_TY, TX, None, None),
        ),
        out_specs=(
            P(SLIDE_TY, TX, None, None),
            P(SLIDE_TY, TX, None, None),
            P(SLIDE_TY_TX, None),
            P("slide", None, None),
            P("slide"),
        ),
        check_vma=False,
    )
```

time: 681 us -> 707 us (1.038)
  waiting for transfers between devices: 191 us -> 403 us
  local copies, waits for them, and re-layouts: 139 us -> 5.05 us
  matrix products: 72.4 us -> 0 us
  Pallas kernels: 0 us -> 45.6 us
  starting transfers between devices: 42.7 us -> 24.2 us
  other arithmetic: 39.7 us -> 23.1 us
  blocking collectives: 179 us -> 191 us
    all_gather x0 -> x1, waiting for transfers between devices: none -> 293 us  [local(): every = lax.all_gather(summary_hidden, TY_TX, axis=0, tiled=True)]
    dot_general x72 -> x0, matrix products: 72.4 us -> none  [the longest x12 14.2 us: head_scores(): jnp.einsum('qhd,khd->hqk', query_heads, key_heads, preferred_element_type...]
    reduce_scatter x4, waiting for transfers between devices: 118 us -> 67.3 us  [own_block(): pieces = lax.psum_scatter(pieces, axes[k], scatter_dimension=0, tiled=True)]
    pallas_call x0 -> x1, Pallas kernels: none -> 45.6 us  [layer(): pl.pallas_call(layer_kernel, out_shape=(jax.ShapeDtypeStruct((rows, width...]
    concatenate x7 -> x0, local copies, waits for them, and re-layouts: 35.7 us -> none  [the longest x3 14.9 us: local(): jnp.concatenate([ungrouped(results[4]), ungrouped(results[5])], axis=1)]
    dynamic_slice x37 -> x1, local copies, waits for them, and re-layouts: 27.9 us -> 0.09 us  [local(): lax.dynamic_slice(count_pad, (grid_row, grid_col), (3, 3)).reshape(NEAR)]
    transpose x5 -> x0, local copies, waits for them, and re-layouts: 26.8 us -> none  [the longest x4 23.6 us: ungrouped(): return stacked.transpose(1, 0, 2).reshape(stacked.shape[1], -1)]
    dynamic_update_slice x24 -> x0, local copies, waits for them, and re-layouts: 21.6 us -> none  [the longest x18 17.7 us: local(): lax.map(query_group, (query_groups, key_groups, value_groups, grad_groups...]
  transfers between devices with their start and end apart: 14 -> 14, of which waited for: 7 -> 10; matrix products, arithmetic and copies ran while one was open for 12% -> 2% of each run, Pallas kernels for 0% -> 0%
where the time goes in v1:
time: 707 us; the launch traced here: 706 us
  waiting for transfers between devices  403 us (57%)
  blocking collectives  191 us (27%)
  Pallas kernels  45.6 us (6%)
  starting transfers between devices  24.2 us (3%)
  other arithmetic  23.1 us (3%)
  between operations  14.4 us (2%)
    all_gather x1, waiting for transfers between devices, local(): every = lax.all_gather(summary_hidden, TY_TX, axis=0, tiled=True)  293 us
    psum x1, blocking collectives, local(): grad_gain = lax.psum(jnp.sum(gain_part, axis=0), TY_TX)  191 us
    reduce_scatter x4, waiting for transfers between devices, own_block(): pieces = lax.psum_scatter(pieces, axes[k], scatter_dimension=0, tiled=True)  67.3 us
    pallas_call x1, Pallas kernels, layer(): pl.pallas_call(layer_kernel, out_shape=(jax.ShapeDtypeStruct((rows, width...  45.6 us
    ppermute x4, waiting for transfers between devices, passed_along(): return lax.ppermute(array, axis, pairs)  21.6 us
    ppermute x2, waiting for transfers between devices, with_halo(): lax.ppermute(head, axis, [((i + 1) % count, i) for i in range(ends)])  18.4 us
  transfers between devices with their start and end apart: 14, of which 10 were waited for; matrix products, arithmetic and copies ran while one was open for 2% of the time, Pallas kernels for 0%

profile of v1, /device:TPU:0, one launch (start us, length us, event | category | flops | bytes accessed | tf_op | source)
XLA Modules:
  0.0 706.3 jit_solution(6146341855984315075)
XLA Ops:
  7.2 0.0 all-gather.2.cloned.1.call-start
  7.2 0.9 fusion.11
  8.1 0.6 multiply_multiply_fusion.1
  8.7 0.5 copy-done.8
  9.2 1.4 fusion.13
  10.6 0.0 reduce-scatter.5.cloned.1.call-start
  10.7 1.1 fusion
  11.8 1.1 multiply_convert_fusion
  12.9 1.3 collective-permute-start.1
  14.2 6.1 collective-permute-start
  20.3 5.3 collective-permute-done.1
  25.6 0.9 collective-permute-done
  26.4 0.1 pad_maximum_fusion.1
  26.5 1.3 collective-permute-start.3
  27.8 4.6 collective-permute-start.2
  32.5 0.1 pad_dynamic-slice_fusion
  32.5 0.1 reshape.94
  32.6 0.6 slice.26
  33.2 0.7 fusion.19
  33.9 0.7 bitcast_select_fusion
  34.6 1.2 pad_add_fusion.meta
  35.8 13.1 %collective-permute-done.3 = bf16[1,3,192,768]{3,2,1,0:T(8,128)(2,1)S(1)} collective-permute-done((bf16[1,3,192,768]{3,2,1,0:T(8,128)(2,1)S(1)}, bf16[1,3,192,768]{3,2,1,0:T(8,128)(2,1)S(1)}, u32[]{:S(2)}, u32[]{:S(2)}) %collective-permute-start.3) | collective-permute-done | bytes 884768 | tf_op jit(solution)/shard_map/ppermute | solution.py:38
  48.9 1.2 collective-permute-done.2
  50.1 1.7 pad_maximum_fusion
  51.7 293.4 %all-gather.2.cloned.1.call-done.summ = bf16[1024,768]{1,0:T(8,128)(2,1)} async-done(((bf16[16,768]{1,0:T(8,128)(2,1)}), bf16[1024,768]{1,0:T(8,128)(2,1)}) %all-gather.2.cloned.1.call-update) | async-done | bytes 1572880 | tf_op jit(solution)/shard_map/all_gather | solution.py:316
  345.2 45.6 %layer.1 = (bf16[192,768]{1,0:T(8,128)(2,1)}, bf16[9,192,768]{2,1,0:T(8,128)(2,1)}, f32[192,768]{1,0:T(8,128)}, bf16[1024,768]{1,0:T(8,128)(2,1)}, bf16[4,768,768]{2,1,0:T(8,128)(2,1)}, /*index=5*/f32[8,768]{1,0:T(8,128)}) custom-call(s32[18]{0:T(128)} %pad_add_fusion.meta, bf16[9,192,768]{2,1,0:T(8,128)(2,1)} %bitcast.37, ...), custom_call_target="tpu_custom_call" | custom-call | tf_op jit(solution)/shard_map/layer/pallas_call | solution.py:266
  390.8 2.8 copy.13
  393.6 0.0 reduce-scatter.7.cloned.1.call-start
  393.6 29.6 %reduce-scatter.5.cloned.1.call-done = bf16[16,16,768]{2,1,0:T(8,128)(2,1)} async-done(((bf16[64,16,768]{2,1,0:T(8,128)(2,1)}), bf16[16,16,768]{2,1,0:T(8,128)(2,1)}) %reduce-scatter.5.cloned.1.call-update) | async-done | bytes 393232 | tf_op jit(solution)/shard_map/reduce_scatter | solution.py:57
  423.3 23.3 %reduce-scatter.7.cloned.1.call-done = bf16[4,16,768]{2,1,0:T(8,128)(2,1)} async-done(((bf16[16,16,768]{2,1,0:T(8,128)(2,1)}), bf16[4,16,768]{2,1,0:T(8,128)(2,1)}) %reduce-scatter.7.cloned.1.call-update) | async-done | bytes 98320 | tf_op jit(solution)/shard_map/reduce_scatter | solution.py:57
  446.7 14.4 %reduce-scatter.9.cloned.1.call-done = bf16[2,16,768]{2,1,0:T(8,128)(2,1)} async-done(((bf16[4,16,768]{2,1,0:T(8,128)(2,1)}), bf16[2,16,768]{2,1,0:T(8,128)(2,1)}) %reduce-scatter.9.cloned.1.call-update) | async-done | bytes 49168 | tf_op jit(solution)/shard_map/reduce_scatter | solution.py:57
  461.1 0.5 all-reduce.3.cloned.1.call-update
  461.6 0.1 fusion.22
  461.8 3.5 collective-permute-start.4
  465.3 1.4 collective-permute-start.5
  466.7 17.2 %collective-permute-done.4 = bf16[3,192,768]{2,1,0:T(8,128)(2,1)S(1)} collective-permute-done((bf16[3,192,768]{2,1,0:T(8,128)(2,1)S(1)}, bf16[3,192,768]{2,1,0:T(8,128)(2,1)S(1)}, u32[]{:S(2)}, u32[]{:S(2)}) %collective-permute-start.4) | collective-permute-done | bytes 884768 | tf_op jit(solution)/shard_map/ppermute | solution.py:48
  483.9 4.3 collective-permute-done.5
  488.3 1.6 fusion.21
  489.9 0.8 slice_bitcast_fusion.2
  490.8 4.6 collective-permute-start.6
  495.4 1.3 collective-permute-start.7
  496.7 190.7 %psum.15 = f32[768]{0:T(1024)S(1)} all-reduce(f32[768]{0:T(1024)S(1)} %reduce_sum.49), channel_id=1, replica_groups=mesh['ty_0'=2,'ty_1'=4,'tx_0'=4,'tx_1'=2,'slide'=2] {'ty_0','ty_1','tx_0..., use_global_device_ids=true, to_apply=%region_10.11 | all-reduce | flops 768 | bytes 6144 | tf_op jit(solution)/shard_map/psum | solution.py:342
  687.4 0.6 div.19
  688.0 1.2 fusion.5
  689.3 0.9 fusion.10
  690.2 0.9 fusion.17
  691.1 1.4 fusion.16
  692.6 6.9 convert_element_type.84
  (37 shorter events, 0.3 us)
Async XLA Ops:
  7.2 25.3 %copy-start.7 = (s32[8,8]{1,0:T(8,128)S(1)}, s32[8,8]{1,0:T(8,128)}, u32[]{:S(2)}) copy-start(s32[8,8]{1,0:T(8,128)} %param.10) | copy-start | bytes 772
  7.2 338.0 %all-gather.2.cloned.1.call-start = ((), (), s32[]{:S(2)}) async-start(), calls=%async_computation.4 | async-start | bytes 1597440 | tf_op jit(solution)/shard_map/all_gather | solution.py:316
  8.7 0.5 copy-start.8
  10.6 412.6 %reduce-scatter.5.cloned.1.call-start = ((), (), s32[]{:S(2)}) async-start(), calls=%async_computation.5 | async-start | bytes 1966080 | tf_op jit(solution)/shard_map/reduce_scatter | solution.py:57
  12.9 12.6 %collective-permute-start.1 = (bf16[1,1,192,768]{3,2,1,0:T(8,128)(2,1)S(1)}, bf16[1,1,192,768]{3,2,1,0:T(8,128)(2,1)S(1)}, u32[]{:S(2)}, u32[]{:S(2)}) collective-permute-start(bf16[1,1,192,768]{3,2,1,0:T(8,128)(2,1)S(1)} %multiply_convert_fusion), channel_id=1, source_target_pairs={{2,0},{4,2},{6,4},{8,6},{10,8},{12,10},{14,12},{3,1},{5,3},{7,5},{... | collective-permute-start | bytes 884744 | tf_op jit(solution)/shard_map/ppermute | solution.py:38
  14.2 12.2 %collective-permute-start = (bf16[1,1,192,768]{3,2,1,0:T(8,128)(2,1)S(1)}, bf16[1,1,192,768]{3,2,1,0:T(8,128)(2,1)S(1)}, u32[]{:S(2)}, u32[]{:S(2)}) collective-permute-start(bf16[1,1,192,768]{3,2,1,0:T(8,128)(2,1)S(1)} %multiply_convert_fusion), channel_id=1, source_target_pairs={{0,2},{2,4},{4,6},{6,8},{8,10},{10,12},{12,14},{1,3},{3,5},{5,7},{... | collective-permute-start | bytes 884744 | tf_op jit(solution)/shard_map/ppermute | solution.py:36
  26.5 22.4 %collective-permute-start.3 = (bf16[1,3,192,768]{3,2,1,0:T(8,128)(2,1)S(1)}, bf16[1,3,192,768]{3,2,1,0:T(8,128)(2,1)S(1)}, u32[]{:S(2)}, u32[]{:S(2)}) collective-permute-start(bf16[1,3,192,768]{3,2,1,0:T(8,128)(2,1)S(1)} %pad_maximum_fusion.1), channel_id=1, source_target_pairs={{16,0},{32,16},{48,32},{64,48},{80,64},{96,80},{112,96},{17,1},{33... | collective-permute-start | bytes 2654216 | tf_op jit(solution)/shard_map/ppermute | solution.py:38
  27.8 22.3 %collective-permute-start.2 = (bf16[1,3,192,768]{3,2,1,0:T(8,128)(2,1)S(1)}, bf16[1,3,192,768]{3,2,1,0:T(8,128)(2,1)S(1)}, u32[]{:S(2)}, u32[]{:S(2)}) collective-permute-start(bf16[1,3,192,768]{3,2,1,0:T(8,128)(2,1)S(1)} %pad_maximum_fusion.1), channel_id=1, source_target_pairs={{0,16},{16,32},{32,48},{48,64},{64,80},{80,96},{96,112},{1,17},{17... | collective-permute-start | bytes 2654216 | tf_op jit(solution)/shard_map/ppermute | solution.py:36
  393.6 68.1 %copy-start.1 = (bf16[9,192,768]{2,1,0:T(8,128)(2,1)S(1)}, bf16[9,192,768]{2,1,0:T(8,128)(2,1)}, u32[]{:S(2)}) copy-start(bf16[9,192,768]{2,1,0:T(8,128)(2,1)} %get-tuple-element.13) | copy-start | bytes 7962628
  393.6 53.0 %reduce-scatter.7.cloned.1.call-start = ((), (), s32[]{:S(2)}) async-start(), calls=%async_computation.6 | async-start | bytes 491520 | tf_op jit(solution)/shard_map/reduce_scatter | solution.py:57
  423.3 37.7 %reduce-scatter.9.cloned.1.call-start = ((), (), s32[]{:S(2)}) async-start(), calls=%async_computation.7 | async-start | bytes 147456 | tf_op jit(solution)/shard_map/reduce_scatter | solution.py:57
  446.6 243.6 %reduce-scatter.11.cloned.1.call-start = ((), (), s32[]{:S(2)}) async-start(), calls=%async_computation.8 | async-start | bytes 73728 | tf_op jit(solution)/shard_map/reduce_scatter | solution.py:57
  461.1 231.5 %all-reduce.3.cloned.1.call-start = ((), (), s32[]{:S(2)}) async-start(), calls=%async_computation.9 | async-start | bytes 9437184 | tf_op jit(solution)/shard_map/psum | solution.py:341
  461.8 22.1 %collective-permute-start.4 = (bf16[3,192,768]{2,1,0:T(8,128)(2,1)S(1)}, bf16[3,192,768]{2,1,0:T(8,128)(2,1)S(1)}, u32[]{:S(2)}, u32[]{:S(2)}) collective-permute-start(bf16[3,192,768]{2,1,0:T(8,128)(2,1)S(1)} %get-tuple-element.21), channel_id=1, source_target_pairs={{0,16},{16,32},{32,48},{48,64},{64,80},{80,96},{96,112},{1,17},{17... | collective-permute-start | bytes 2654216 | tf_op jit(solution)/shard_map/ppermute | solution.py:48
  465.2 31.5 %copy-start.6 = (f32[8,768]{1,0:T(8,128)S(1)}, f32[8,768]{1,0:T(8,128)}, u32[]{:S(2)}) copy-start(f32[8,768]{1,0:T(8,128)} %get-tuple-element.16) | copy-start | bytes 73732
  465.2 222.2 %copy-start.5 = (f32[768]{0:T(1024)S(1)}, f32[768]{0:T(1024)}, u32[]{:S(2)}) copy-start(f32[768]{0:T(1024)} %param.13) | copy-start | bytes 9220
  465.3 222.8 %copy-start = (bf16[1,1,192,768]{3,2,1,0:T(8,128)(2,1)S(1)}, bf16[1,1,192,768]{3,2,1,0:T(8,128)(2,1)}, u32[]{:S(2)}) copy-start(bf16[1,1,192,768]{3,2,1,0:T(8,128)(2,1)} %param.8) | copy-start | bytes 884740
  465.3 222.8 %copy-start.3 = (f32[192,768]{1,0:T(8,128)S(1)}, f32[192,768]{1,0:T(8,128)}, u32[]{:S(2)}) copy-start(f32[192,768]{1,0:T(8,128)} %get-tuple-element.12) | copy-start | bytes 1769476
  465.3 23.0 %collective-permute-start.5 = (bf16[3,192,768]{2,1,0:T(8,128)(2,1)S(1)}, bf16[3,192,768]{2,1,0:T(8,128)(2,1)S(1)}, u32[]{:S(2)}, u32[]{:S(2)}) collective-permute-start(bf16[3,192,768]{2,1,0:T(8,128)(2,1)S(1)} %get-tuple-element.22), channel_id=1, source_target_pairs={{16,0},{32,16},{48,32},{64,48},{80,64},{96,80},{112,96},{17,1},{33... | collective-permute-start | bytes 2654216 | tf_op jit(solution)/shard_map/ppermute | solution.py:48
  489.9 199.4 %copy-start.2 = (bf16[1,1,192,768]{3,2,1,0:T(8,128)(2,1)S(1)}, bf16[1,1,192,768]{3,2,1,0:T(8,128)(2,1)}, u32[]{:S(2)}) copy-start(bf16[1,1,192,768]{3,2,1,0:T(8,128)(2,1)} %param.15) | copy-start | bytes 884740
  489.9 200.3 %copy-start.4 = (bf16[16,768]{1,0:T(8,128)(2,1)S(1)}, bf16[16,768]{1,0:T(8,128)(2,1)}, u32[]{:S(2)}) copy-start(bf16[16,768]{1,0:T(8,128)(2,1)} %param.9) | copy-start | bytes 73732
  489.9 201.2 %copy-start.9 = (f32[16]{0:T(128)S(1)}, f32[16]{0:T(128)}, u32[]{:S(2)}) copy-start(f32[16]{0:T(128)} %copy-done.8) | copy-start | bytes 196
  489.9 201.2 %copy-start.10 = (f32[16]{0:T(128)S(1)}, f32[16]{0:T(128)}, u32[]{:S(2)}) copy-start(f32[16]{0:T(128)} %get-tuple-element.27) | copy-start | bytes 196
  490.8 197.2 %collective-permute-start.6 = (bf16[192,768]{1,0:T(8,128)(2,1)}, bf16[192,768]{1,0:T(8,128)(2,1)S(1)}, u32[]{:S(2)}, u32[]{:S(2)}) collective-permute-start(bf16[192,768]{1,0:T(8,128)(2,1)} %get-tuple-element.23), channel_id=1, source_target_pairs={{0,2},{2,4},{4,6},{6,8},{8,10},{10,12},{12,14},{1,3},{3,5},{5,7},{... | collective-permute-start | bytes 884744 | tf_op jit(solution)/shard_map/ppermute | solution.py:48
  495.4 192.6 %collective-permute-start.7 = (bf16[192,768]{1,0:T(8,128)(2,1)}, bf16[192,768]{1,0:T(8,128)(2,1)}, u32[]{:S(2)}, u32[]{:S(2)}) collective-permute-start(bf16[192,768]{1,0:T(8,128)(2,1)} %get-tuple-element.24), channel_id=1, source_target_pairs={{2,0},{4,2},{6,4},{8,6},{10,8},{12,10},{14,12},{3,1},{5,3},{7,5},{... | collective-permute-start | bytes 884744 | tf_op jit(solution)/shard_map/ppermute | solution.py:48
Sparse Core Ops, SparseCore 0:
  10.8 334.3 all-gather.1
  393.7 29.5 reduce-scatter.4
  425.7 20.8 reduce-scatter.6
  448.9 12.1 reduce-scatter.8
  463.3 14.8 reduce-scatter.10
  484.3 151.8 all-reduce.2

commit v2 on v1

--- a/solution.py
+++ b/solution.py
@@ -21,41 +21,363 @@
 SLIDE_TY_TX = ("slide", "ty_0", "ty_1", "tx_0", "tx_1")
 F32 = jnp.float32
 BF16 = jnp.bfloat16
+MESH = pl.DeviceIdType.MESH
 
 epsilon = 1e-05
 
 
-def with_halo(cells, sides, width):
-    for axis, dim in sides:
-        count = lax.axis_size(axis)
-        ends = count - 1
-        head = lax.slice_in_dim(cells, 0, width, axis=dim)
-        tail = lax.slice_in_dim(cells, cells.shape[dim] - width, cells.shape[dim], axis=dim)
-        cells = jnp.concatenate(
-            [
-                lax.ppermute(tail, axis, [(i, (i + 1) % count) for i in range(ends)]),
-                cells,
-                lax.ppermute(head, axis, [((i + 1) % count, i) for i in range(ends)]),
-            ],
-            axis=dim,
-        )
-    return cells
-
-
-def passed_along(array, axis, by):
-    peers = lax.axis_size(axis)
-    pairs = [(i, i + by) for i in range(peers) if 0 <= i + by < peers]
-    return lax.ppermute(array, axis, pairs)
-
-
-def own_block(pieces, axes, turns):
-    lengths = [lax.axis_size(a) for a in axes]
-    pieces = pieces.reshape(*lengths, *pieces.shape[1:])
-    pieces = pieces.transpose(*turns, *range(len(axes), pieces.ndim))
-    pieces = pieces.reshape(-1, *pieces.shape[len(axes) :])
-    for k in turns:
-        pieces = lax.psum_scatter(pieces, axes[k], scatter_dimension=0, tiled=True)
-    return pieces[0]
+def places():
+    return (
+        2 * lax.axis_index("tx_1") + lax.axis_index("ty_0"),
+        lax.axis_index("ty_1"),
+        lax.axis_index("tx_0"),
+    )
+
+
+def peer(axis, at, by):
+    there = lax.rem(at[axis] + (by + 4), 4)
+    if axis == 0:
+        return {"tx_1": there // 2, "ty_0": lax.rem(there, 2)}
+    return {"ty_1": there} if axis == 1 else {"tx_0": there}
+
+
+def row_peer(at, by):
+    there = lax.rem(lax.axis_index("ty_0") * 4 + at[1] + (by + 8), 8)
+    return {"ty_0": there // 4, "ty_1": lax.rem(there, 4)}
+
+
+def greet(at):
+    barrier = pltpu.get_barrier_semaphore()
+    others = [peer(axis, at, by) for axis in range(3) for by in (1, 2, 3)]
+    others += [row_peer(at, 1), row_peer(at, -1)]
+    for other in others:
+        pl.semaphore_signal(barrier, inc=1, device_id=other, device_id_type=MESH)
+    pl.semaphore_wait(barrier, len(others))
+
+
+class Sender:
+    def __init__(self, send_sems, recv_sems):
+        self.send_sems, self.recv_sems = send_sems, recv_sems
+        self.copies = []
+
+    def send(self, src, dst, device):
+        k = len(self.copies)
+        copy = pltpu.make_async_remote_copy(
+            src_ref=src,
+            dst_ref=dst,
+            send_sem=self.send_sems.at[k],
+            recv_sem=self.recv_sems.at[k],
+            device_id=device,
+            device_id_type=MESH,
+        )
+        copy.start()
+        self.copies.append(copy)
+        return copy
+
+    def drain(self):
+        for copy in self.copies:
+            copy.wait_send()
+
+
+def take_turns(tasks):
+    tasks = list(tasks)
+    while tasks:
+        tasks = [task for task in tasks if next(task, "end") != "end"]
+
+
+def added(*refs):
+    total = refs[0][...].astype(F32)
+    for ref in refs[1:]:
+        total = total + ref[...].astype(F32)
+    return total
+
+
+def scatter_ring(link, axis, at, piece, relay, direct, out):
+    c = at[axis]
+    right, left, across = [lax.rem(c + k, 4) for k in (1, 3, 2)]
+    to_right, to_left = peer(axis, at, 1), peer(axis, at, -1)
+    far_a = link.send(piece(across, 0), relay.at[0, 0], to_right)
+    far_b = link.send(piece(across, 1), relay.at[0, 1], to_left)
+    near_b = link.send(piece(right, 1), direct.at[0, 1], to_right)
+    near_a = link.send(piece(left, 0), direct.at[1, 0], to_left)
+    yield
+    far_a.wait_recv()
+    relay[1, 0] = added(relay.at[0, 0], piece(right, 0)).astype(BF16)
+    sum_a = link.send(relay.at[1, 0], direct.at[0, 0], to_right)
+    yield
+    far_b.wait_recv()
+    relay[1, 1] = added(relay.at[0, 1], piece(left, 1)).astype(BF16)
+    sum_b = link.send(relay.at[1, 1], direct.at[1, 1], to_left)
+    yield
+    for copy in (near_b, near_a, sum_a, sum_b):
+        copy.wait_recv()
+    for half in range(2):
+        out[half] = added(piece(c, half), direct.at[0, half], direct.at[1, half]).astype(BF16)
+
+
+def scatter_direct(link, axis, at, piece, slots, out):
+    copies = [
+        link.send(piece(lax.rem(at[axis] + k, 4)), slots.at[k - 1], peer(axis, at, k))
+        for k in (1, 3, 2)
+    ]
+    yield
+    for copy in copies:
+        copy.wait_recv()
+    total = added(piece(at[axis]), slots.at[0], slots.at[1], slots.at[2])
+    out[...] = total.astype(out.dtype)
+
+
+def gather_direct(link, axis, at, place):
+    mine = place(at[axis])
+    copies = [link.send(mine, mine, peer(axis, at, k)) for k in (1, 3, 2)]
+    yield
+    for copy in copies:
+        copy.wait_recv()
+
+
+def gather_ring(link, axis, at, place, half_place):
+    c = at[axis]
+    right, left = lax.rem(c + 1, 4), lax.rem(c + 3, 4)
+    to_right, to_left = peer(axis, at, 1), peer(axis, at, -1)
+    mine = place(c)
+    one = link.send(mine, mine, to_right)
+    two = link.send(mine, mine, to_left)
+    yield
+    one.wait_recv()
+    half = half_place(left, 0)
+    three = link.send(half, half, to_right)
+    yield
+    two.wait_recv()
+    half = half_place(right, 1)
+    four = link.send(half, half, to_left)
+    yield
+    three.wait_recv()
+    four.wait_recv()
+
+
+def gather_kernel(hidden, summ, near, every, send_sems, recv_sems):
+    at = places()
+    x, y, z = at
+    x_hi, x_lo = lax.axis_index("tx_1"), lax.axis_index("ty_0")
+    near[1, 1] = hidden[...]
+    every[x_lo, y, z, x_hi] = summ[...]
+    greet(at)
+    link = Sender(send_sems, recv_sems)
+    from_x, from_z = 2 - 2 * x_hi, 2 * x_hi
+
+    def halo():
+        beside = link.send(hidden, near.at[1, 2 * x_hi], {"tx_1": 1 - x_hi})
+        rows = [
+            link.send(hidden, near.at[0, 1], row_peer(at, 1)),
+            link.send(hidden, near.at[2, 1], row_peer(at, -1)),
+        ]
+        yield
+        beside.wait_recv()
+        there = {"tx_0": lax.rem(z + (5 - 2 * x_hi), 4)}
+        beyond = link.send(near.at[1, from_x], near.at[1, from_z], there)
+        rows.append(link.send(near.at[1, from_x], near.at[0, from_x], row_peer(at, 1)))
+        rows.append(link.send(near.at[1, from_x], near.at[2, from_x], row_peer(at, -1)))
+        yield
+        beyond.wait_recv()
+        rows.append(link.send(near.at[1, from_z], near.at[0, from_z], row_peer(at, 1)))
+        rows.append(link.send(near.at[1, from_z], near.at[2, from_z], row_peer(at, -1)))
+        yield
+        yield
+        yield
+        for copy in rows:
+            copy.wait_recv()
+
+    def summaries():
+        yield from gather_direct(link, 1, at, lambda d: every.at[x_lo, d, z, x_hi])
+        yield from gather_direct(
+            link, 0, at, lambda d: every.at[lax.rem(d, 2), :, z, d // 2]
+        )
+        yield from gather_ring(
+            link, 2, at, lambda d: every.at[:, :, d], lambda d, half: every.at[half, :, d]
+        )
+
+    take_turns([summaries(), halo()])
+    link.drain()
+
+
+def gather(hidden, summary_hidden):
+    rows, width = hidden.shape
+    block = summary_hidden.shape[0]
+    vm = pl.BlockSpec(memory_space=pltpu.VMEM)
+    sends = 3 + 3 + 4 + 3 + 3 + 2
+    near, every = pl.pallas_call(
+        gather_kernel,
+        out_shape=(
+            jax.ShapeDtypeStruct((3, 3, rows, width), BF16),
+            jax.ShapeDtypeStruct((2, 4, 4, 2, block, width), BF16),
+        ),
+        in_specs=[vm] * 2,
+        out_specs=(vm,) * 2,
+        scratch_shapes=[
+            pltpu.SemaphoreType.DMA((sends,)),
+            pltpu.SemaphoreType.DMA((sends,)),
+        ],
+        compiler_params=pltpu.CompilerParams(
+            collective_id=0, has_side_effects=True, vmem_limit_bytes=32 * 1024 * 1024
+        ),
+        name="gather",
+    )(hidden, summary_hidden)
+    return near.reshape(NEAR, rows, width), every.reshape(-1, width)
+
+
+def exchange_kernel(
+    near, own, sums, w_in, gain, out_own, out_sum, w_out, out_gain,
+    beside, row_sum, z_slot, x_slot, message,
+    s_relay, s_direct, s_one, s_slots_x, s_two, s_slots_y,
+    w_relay, w_direct, w_one, w_slots_two, w_two, w_slots_three,
+    gain_sum, gain_slots, send_sems, recv_sems,
+):
+    at = places()
+    x, y, z = at
+    x_hi = lax.axis_index("tx_1")
+    greet(at)
+    link = Sender(send_sems, recv_sems)
+
+    def halo():
+        rows = []
+        for j in (0, 2, 1):
+            up = link.send(near.at[2, j], beside.at[0, j], row_peer(at, 1))
+            down = link.send(near.at[0, j], beside.at[1, j], row_peer(at, -1))
+            rows.append((j, up, down))
+        yield
+        for j, up, down in rows[:2]:
+            up.wait_recv()
+            down.wait_recv()
+            row_sum[j // 2] = added(near.at[1, j], beside.at[0, j], beside.at[1, j]).astype(BF16)
+        there = {"tx_0": lax.rem(z + (3 + 2 * x_hi), 4)}
+        far = link.send(row_sum.at[x_hi], z_slot, there)
+        yield
+        _, up, down = rows[2]
+        up.wait_recv()
+        down.wait_recv()
+        out_own[...] = own[...] + added(beside.at[0, 1], beside.at[1, 1])
+        far.wait_recv()
+        message[...] = added(row_sum.at[1 - x_hi], z_slot).astype(BF16)
+        last = link.send(message, x_slot, {"tx_1": 1 - x_hi})
+        yield
+        yield
+        last.wait_recv()
+        out_own[...] += x_slot[...].astype(F32)
+
+    def summaries():
+        half = sums.shape[0] // 2
+        yield from scatter_ring(
+            link, 2, at, lambda d, h: sums.at[pl.ds(h * half, half), d], s_relay, s_direct, s_one
+        )
+        block = out_sum.shape[0]
+        yield from scatter_direct(
+            link, 0, at,
+            lambda d: s_one.at[lax.rem(d, 2), :, pl.ds((d // 2) * block, block)],
+            s_slots_x, s_two,
+        )
+        yield from scatter_direct(link, 1, at, lambda d: s_two.at[d], s_slots_y, out_sum)
+
+    def weights(p):
+        a, b, c = p, (p + 1) % 3, (p + 2) % 3
+        part = w_in.shape[0] // 3
+        size = [part // 4, part // 16, part // 64]
+        first = p * part
+
+        def rows_of(ref, start, count):
+            return ref.at[pl.ds(pl.multiple_of(start, PACK), count)]
+
+        yield from scatter_ring(
+            link, a, at,
+            lambda d, h: rows_of(w_in, first + d * size[0] + h * (size[0] // 2), size[0] // 2),
+            w_relay.at[p], w_direct.at[p], w_one.at[p],
+        )
+        yield from scatter_direct(
+            link, b, at,
+            lambda d: w_one.at[p, d // 2, pl.ds(lax.rem(d, 2) * size[1], size[1])],
+            w_slots_two.at[p], w_two.at[p],
+        )
+        base = first + at[a] * size[0]
+        inner = base + at[b] * size[1]
+        yield from scatter_direct(
+            link, c, at,
+            lambda d: rows_of(w_two.at[p], d * size[2], size[2]),
+            w_slots_three.at[p],
+            rows_of(w_out, inner + at[c] * size[2], size[2]),
+        )
+        yield from gather_direct(
+            link, c, at, lambda d: rows_of(w_out, inner + d * size[2], size[2])
+        )
+        yield from gather_direct(
+            link, b, at, lambda d: rows_of(w_out, base + d * size[1], size[1])
+        )
+        yield from gather_ring(
+            link, a, at,
+            lambda d: rows_of(w_out, first + d * size[0], size[0]),
+            lambda d, h: rows_of(
+                w_out, first + d * size[0] + h * (size[0] // 2), size[0] // 2
+            ),
+        )
+
+    def gains():
+        gain_sum[0] = gain[...]
+        for k in range(3):
+            yield from scatter_direct(
+                link, k, at, lambda d, k=k: gain_sum.at[k], gain_slots.at[k],
+                gain_sum.at[k + 1] if k < 2 else out_gain,
+            )
+
+    take_turns([halo(), summaries(), weights(0), weights(1), weights(2), gains()])
+    link.drain()
+
+
+def exchange(near_grad, own_grad, sum_grad, w_part, gain_part, block):
+    rows, width = own_grad.shape
+    vm = pl.BlockSpec(memory_space=pltpu.VMEM)
+    total = w_part.shape[0] * width
+    part = total // 3
+    sends = 6 + 2 + 6 + 3 + 3 + 3 * (6 + 3 + 3 + 3 + 3 + 4) + 9
+    sums = sum_grad.reshape(8, 4, 2 * block, width)
+    own, sum_own, w_all, gain = pl.pallas_call(
+        exchange_kernel,
+        out_shape=(
+            jax.ShapeDtypeStruct((rows, width), F32),
+            jax.ShapeDtypeStruct((block, width), F32),
+            jax.ShapeDtypeStruct((total, width), BF16),
+            jax.ShapeDtypeStruct((8, width), F32),
+        ),
+        in_specs=[vm] * 5,
+        out_specs=(vm,) * 4,
+        scratch_shapes=[
+            pltpu.VMEM((2, 3, rows, width), BF16),
+            pltpu.VMEM((2, rows, width), BF16),
+            pltpu.VMEM((rows, width), BF16),
+            pltpu.VMEM((rows, width), BF16),
+            pltpu.VMEM((rows, width), BF16),
+            pltpu.VMEM((2, 2, 4, 2 * block, width), BF16),
+            pltpu.VMEM((2, 2, 4, 2 * block, width), BF16),
+            pltpu.VMEM((2, 4, 2 * block, width), BF16),
+            pltpu.VMEM((3, 4, block, width), BF16),
+            pltpu.VMEM((4, block, width), BF16),
+            pltpu.VMEM((3, block, width), BF16),
+            pltpu.VMEM((3, 2, 2, part // 8, width), BF16),
+            pltpu.VMEM((3, 2, 2, part // 8, width), BF16),
+            pltpu.VMEM((3, 2, part // 8, width), BF16),
+            pltpu.VMEM((3, 3, part // 16, width), BF16),
+            pltpu.VMEM((3, part // 16, width), BF16),
+            pltpu.VMEM((3, 3, part // 64, width), BF16),
+            pltpu.VMEM((3, 8, width), F32),
+            pltpu.VMEM((3, 3, 8, width), F32),
+            pltpu.SemaphoreType.DMA((sends,)),
+            pltpu.SemaphoreType.DMA((sends,)),
+        ],
+        compiler_params=pltpu.CompilerParams(
+            collective_id=1, has_side_effects=True, vmem_limit_bytes=48 * 1024 * 1024
+        ),
+        name="exchange",
+    )(
+        near_grad.reshape(3, 3, rows, width), own_grad, sums, w_part.reshape(total, width), gain_part
+    )
+    return own, sum_own, w_all.reshape(w_part.shape), jnp.sum(gain, axis=0)
 
 
 def normalize(rows, gain):
@@ -313,9 +635,7 @@
     grads_in = cotangent[0, 0]
     hidden, row_scale = normalize(token_rows, norm_gain)
     summary_hidden, summary_scale = normalize(summary, norm_gain)
-    every = lax.all_gather(summary_hidden, TY_TX, axis=0, tiled=True)
-    near = with_halo(hidden.reshape(1, 1, rows, width), ((TX, 1), (TY, 0)), 1)
-    near = near.reshape(NEAR, rows, width)
+    near, every = gather(hidden, summary_hidden)
     count_pad = jnp.pad(counts, 1)
     near_counts = lax.dynamic_slice(count_pad, (grid_row, grid_col), (3, 3)).reshape(NEAR)
     flags = lax.dynamic_slice(tile_pattern, (grid_row, grid_col, zero), (1, 1, NEAR)).reshape(NEAR)
@@ -329,17 +649,10 @@
     updated, near_grad, own_grad, sum_grad, w_part, gain_part = layer(
         meta, near, every, projections, token_rows, grads_in
     )
-    near_grad = near_grad.reshape(3, 3, rows, width)
-    row_lower = passed_along(near_grad[2], TY, 1).astype(F32)
-    row_upper = passed_along(near_grad[0], TY, -1).astype(F32)
-    row_sum = near_grad[1].astype(F32) + row_lower + row_upper
-    from_lower = passed_along(row_sum[2].astype(BF16), TX, 1).astype(F32)
-    from_upper = passed_along(row_sum[0].astype(BF16), TX, -1).astype(F32)
-    hidden_grad = own_grad + row_sum[1] + from_lower + from_upper
-    pieces = sum_grad.reshape(-1, summary.shape[0], width)
-    summary_hidden_grad = own_block(pieces, TY_TX, (1, 2, 0, 3)).astype(F32)
-    grad_proj = lax.psum(w_part, TY_TX).astype(F32)
-    grad_gain = lax.psum(jnp.sum(gain_part, axis=0), TY_TX)
+    hidden_grad, summary_hidden_grad, grad_proj, grad_gain = exchange(
+        near_grad, own_grad, sum_grad, w_part, gain_part, summary.shape[0]
+    )
+    grad_proj = grad_proj.astype(F32)
     grad_gain = grad_gain / norm_gain
     grad_tokens = (
         grads_in.astype(F32) + norm_back(token_rows, row_scale, norm_gain, hidden_grad)

time: 707 us -> 213 us (0.30)
  waiting for transfers between devices: 403 us -> 0 us
  blocking collectives: 191 us -> 0 us
  Pallas kernels: 45.6 us -> 187 us
  starting transfers between devices: 24.2 us -> 0 us
  between operations: 14.4 us -> 0.72 us
  other arithmetic: 23.1 us -> 15.9 us
    all_gather x1 -> x0, waiting for transfers between devices: 293 us -> none  [local(): every = lax.all_gather(summary_hidden, TY_TX, axis=0, tiled=True)]
    psum x1 -> x0, blocking collectives: 191 us -> none  [local(): grad_gain = lax.psum(jnp.sum(gain_part, axis=0), TY_TX)]
    pallas_call x0 -> x2, Pallas kernels: none -> 141 us  [the longest x1 98.3 us: exchange(): pl.pallas_call(exchange_kernel, out_shape=(jax.ShapeDtypeStruct((rows, wi...]
    reduce_scatter x4 -> x0, waiting for transfers between devices: 67.3 us -> none  [own_block(): pieces = lax.psum_scatter(pieces, axes[k], scatter_dimension=0, tiled=True)]
    ppermute x8 -> x0, waiting for transfers between devices: 42 us -> none  [the longest x4 21.6 us: passed_along(): return lax.ppermute(array, axis, pairs)]
    ppermute x8 -> x0, starting transfers between devices: 24 us -> none  [the longest x4 10.8 us: passed_along(): return lax.ppermute(array, axis, pairs)]
    unnamed x22 -> x20, local copies, waits for them, and re-layouts: 0.59 us -> 7.7 us
  transfers between devices with their start and end apart: 14 -> 0, of which waited for: 10 -> 0; matrix products, arithmetic and copies ran while one was open for 2% -> 0% of each run, Pallas kernels for 0% -> 0%
where the time goes in v2:
time: 213 us; the launch traced here: 212 us
  Pallas kernels  187 us (88%)
  other arithmetic  15.9 us (7%)
  local copies, waits for them, and re-layouts  9.14 us (4%)
    pallas_call x1, Pallas kernels, exchange(): pl.pallas_call(exchange_kernel, out_shape=(jax.ShapeDtypeStruct((rows, wi...  98.3 us
    pallas_call x1, Pallas kernels, layer(): pl.pallas_call(layer_kernel, out_shape=(jax.ShapeDtypeStruct((rows, width...  45.5 us
    pallas_call x1, Pallas kernels, gather(): pl.pallas_call(gather_kernel, out_shape=(jax.ShapeDtypeStruct((3, 3, rows...  42.8 us
    unnamed x20, local copies, waits for them, and re-layouts  7.7 us
    convert_element_type x1, other arithmetic, local(): grad_proj = grad_proj.astype(F32)  6.9 us

profile of v2, /device:TPU:0, one launch (start us, length us, event | category | flops | bytes accessed | tf_op | source)
XLA Modules:
  0.0 212.3 jit_solution(3086459791130466133)
XLA Ops:
  0.6 0.7 fusion.16
  1.3 0.9 fusion.9
  2.2 0.8 pad_dynamic-slice_fusion
  2.9 0.1 reshape.81
  3.0 0.6 slice.3
  3.6 0.7 bitcast_select_fusion
  4.3 1.2 pad_add_fusion.meta
  5.5 1.1 fusion
  6.6 0.8 fusion.11.summ
  7.5 1.1 fusion.2.hidden
  8.6 42.8 %gather.1 = (bf16[3,3,192,768]{3,2,1,0:T(8,128)(2,1)S(1)}, bf16[2,4,4,2,16,768]{5,4,3,2,1,0:T(8,128)(2,1)S(1)}) custom-call(bf16[192,768]{1,0:T(8,128)(2,1)S(1)} %fusion.2.hidden, bf16[16,768]{1,0:T(8,128)(2,1)S(1)} %fusion.11.summ), custom_call_target="tpu_custom_call" | custom-call | tf_op jit(solution)/shard_map/gather/pallas_call | solution.py:208
  51.4 0.0 copy-start
  51.4 1.5 copy-done
  52.9 0.0 copy-start.2
  52.9 1.2 copy-done.2
  54.1 45.5 %layer.1 = (bf16[192,768]{1,0:T(8,128)(2,1)}, bf16[9,192,768]{2,1,0:T(8,128)(2,1)}, f32[192,768]{1,0:T(8,128)}, bf16[1024,768]{1,0:T(8,128)(2,1)}, bf16[4,768,768]{2,1,0:T(8,128)(2,1)}, /*index=5*/f32[8,768]{1,0:T(8,128)}) custom-call(s32[18]{0:T(128)} %pad_add_fusion.meta, bf16[9,192,768]{2,1,0:T(8,128)(2,1)} %bitcast.21, bf16[1024,768]{1,0:T(8,128)(2,1)} %bitcast.23, ...), custom_call_target="tpu_custom_call" | custom-call | tf_op jit(solution)/shard_map/layer/pallas_call | solution.py:588
  99.6 0.0 copy-start.1
  99.6 1.7 copy-done.1
  101.3 0.0 copy-start.3
  101.3 1.4 copy-done.3
  102.7 0.0 copy-start.4
  102.7 1.1 copy-done.4
  103.8 0.0 copy-start.5
  103.8 0.7 copy-done.5
  104.5 0.0 copy-start.8
  104.5 0.0 copy-start.9
  104.5 0.0 copy-start.6
  104.5 0.0 copy-start.7
  104.5 98.3 %exchange.1 = (f32[192,768]{1,0:T(8,128)S(1)}, f32[16,768]{1,0:T(8,128)S(1)}, bf16[3072,768]{1,0:T(8,128)(2,1)}, f32[8,768]{1,0:T(8,128)S(1)}) custom-call(bf16[3,3,192,768]{3,2,1,0:T(8,128)(2,1)S(1)} %bitcast.22, f32[192,768]{1,0:T(8,128)S(1)} %copy-done.4, bf16[8,4,32,768]{3,2,1,0:T(8,128)(2,1)S(1)} %bitcast.24, bf16[3072,768]{1,0:T(8,128)(2,1)} %bitcast.27, ...), custom_call_target="tpu_custom_call" | custom-call | tf_op jit(solution)/shard_map/exchange/pallas_call | solution.py:340
  202.8 0.0 copy-done.8
  202.8 0.0 copy-done.9
  202.9 0.1 fusion.15
  203.0 0.7 fusion.14
  203.7 0.0 copy-done.6
  203.7 0.2 fusion.7
  203.8 0.0 copy-done.7
  203.9 1.0 fusion.8
  204.8 0.6 div.19
  205.4 6.9 %convert.2 = f32[4,768,768]{2,1,0:T(8,128)} convert(bf16[4,768,768]{2,1,0:T(8,128)(2,1)} %bitcast.26) | non-fusion elementwise | flops 2359296 | bytes 14155776 | tf_op jit(solution)/shard_map/convert_element_type | solution.py:655
  (5 shorter events, 0.0 us)
Async XLA Ops:
  51.4 1.5 copy-start
  52.9 1.2 copy-start.2
  99.6 1.8 copy-start.1
  101.3 1.4 copy-start.3
  102.7 1.1 copy-start.4
  103.8 0.7 copy-start.5
  104.5 98.3 %copy-start.8 = (bf16[16,768]{1,0:T(8,128)(2,1)S(1)}, bf16[16,768]{1,0:T(8,128)(2,1)}, u32[]{:S(2)}) copy-start(bf16[16,768]{1,0:T(8,128)(2,1)} %param.9) | copy-start | bytes 73732
  104.5 98.3 %copy-start.9 = (f32[768]{0:T(1024)S(1)}, f32[768]{0:T(1024)}, u32[]{:S(2)}) copy-start(f32[768]{0:T(1024)} %param.13) | copy-start | bytes 9220
  104.5 99.2 %copy-start.6 = (bf16[1,1,192,768]{3,2,1,0:T(8,128)(2,1)S(1)}, bf16[1,1,192,768]{3,2,1,0:T(8,128)(2,1)}, u32[]{:S(2)}) copy-start(bf16[1,1,192,768]{3,2,1,0:T(8,128)(2,1)} %param.8) | copy-start | bytes 884740
  104.5 99.3 %copy-start.7 = (bf16[1,1,192,768]{3,2,1,0:T(8,128)(2,1)S(1)}, bf16[1,1,192,768]{3,2,1,0:T(8,128)(2,1)}, u32[]{:S(2)}) copy-start(bf16[1,1,192,768]{3,2,1,0:T(8,128)(2,1)} %param.15) | copy-start | bytes 884740

commit v3 on v2

--- a/solution.py
+++ b/solution.py
@@ -14,9 +14,7 @@
 CHUNK = 256
 PACK = 16
 NEAR = 9
-TY = ("ty_0", "ty_1")
 TX = ("tx_0", "tx_1")
-TY_TX = ("ty_0", "ty_1", "tx_0", "tx_1")
 SLIDE_TY = ("slide", "ty_0", "ty_1")
 SLIDE_TY_TX = ("slide", "ty_0", "ty_1", "tx_0", "tx_1")
 F32 = jnp.float32
@@ -52,7 +50,18 @@
     others += [row_peer(at, 1), row_peer(at, -1)]
     for other in others:
         pl.semaphore_signal(barrier, inc=1, device_id=other, device_id_type=MESH)
-    pl.semaphore_wait(barrier, len(others))
+    return lambda: pl.semaphore_wait(barrier, len(others))
+
+
+class Loader:
+    def __init__(self, sems):
+        self.sems, self.count = sems, 0
+
+    def copy(self, src, dst):
+        copy = pltpu.make_async_copy(src, dst, self.sems.at[self.count])
+        self.count += 1
+        copy.start()
+        return copy
 
 
 class Sender:
@@ -92,7 +101,7 @@
     return total
 
 
-def scatter_ring(link, axis, at, piece, relay, direct, out):
+def scatter_ring(link, axis, at, piece, held, ready, relay, direct, out):
     c = at[axis]
     right, left, across = [lax.rem(c + k, 4) for k in (1, 3, 2)]
     to_right, to_left = peer(axis, at, 1), peer(axis, at, -1)
@@ -101,18 +110,19 @@
     near_b = link.send(piece(right, 1), direct.at[0, 1], to_right)
     near_a = link.send(piece(left, 0), direct.at[1, 0], to_left)
     yield
+    for copy in ready:
+        copy.wait()
     far_a.wait_recv()
-    relay[1, 0] = added(relay.at[0, 0], piece(right, 0)).astype(BF16)
+    relay[1, 0] = added(relay.at[0, 0], held.at[0]).astype(BF16)
     sum_a = link.send(relay.at[1, 0], direct.at[0, 0], to_right)
-    yield
     far_b.wait_recv()
-    relay[1, 1] = added(relay.at[0, 1], piece(left, 1)).astype(BF16)
+    relay[1, 1] = added(relay.at[0, 1], held.at[1]).astype(BF16)
     sum_b = link.send(relay.at[1, 1], direct.at[1, 1], to_left)
     yield
     for copy in (near_b, near_a, sum_a, sum_b):
         copy.wait_recv()
     for half in range(2):
-        out[half] = added(piece(c, half), direct.at[0, half], direct.at[1, half]).astype(BF16)
+        out[half] = added(held.at[2 + half], direct.at[0, half], direct.at[1, half]).astype(BF16)
 
 
 def scatter_direct(link, axis, at, piece, slots, out):
@@ -146,7 +156,6 @@
     one.wait_recv()
     half = half_place(left, 0)
     three = link.send(half, half, to_right)
-    yield
     two.wait_recv()
     half = half_place(right, 1)
     four = link.send(half, half, to_left)
@@ -155,13 +164,19 @@
     four.wait_recv()
 
 
-def gather_kernel(hidden, summ, near, every, send_sems, recv_sems):
+def gather_kernel(
+    tokens, summary, gain, near, every, hidden, summ, local_sems, send_sems, recv_sems
+):
     at = places()
     x, y, z = at
     x_hi, x_lo = lax.axis_index("tx_1"), lax.axis_index("ty_0")
-    near[1, 1] = hidden[...]
-    every[x_lo, y, z, x_hi] = summ[...]
-    greet(at)
+    met = greet(at)
+    summ[...] = normalize(summary[...], gain[...])[0]
+    hidden[...] = normalize(tokens[...], gain[...])[0]
+    load = Loader(local_sems)
+    own = every.at[x_lo, y, z, x_hi]
+    kept = [load.copy(summ, own), load.copy(hidden, near.at[1, 1])]
+    met()
     link = Sender(send_sems, recv_sems)
     from_x, from_z = 2 - 2 * x_hi, 2 * x_hi
 
@@ -188,7 +203,11 @@
             copy.wait_recv()
 
     def summaries():
-        yield from gather_direct(link, 1, at, lambda d: every.at[x_lo, d, z, x_hi])
+        copies = [link.send(summ, own, peer(1, at, k)) for k in (1, 3, 2)]
+        yield
+        kept[0].wait()
+        for copy in copies:
+            copy.wait_recv()
         yield from gather_direct(
             link, 0, at, lambda d: every.at[lax.rem(d, 2), :, z, d // 2]
         )
@@ -197,12 +216,13 @@
         )
 
     take_turns([summaries(), halo()])
+    kept[1].wait()
     link.drain()
 
 
-def gather(hidden, summary_hidden):
-    rows, width = hidden.shape
-    block = summary_hidden.shape[0]
+def gather(tokens, summary, gain):
+    rows, width = tokens.shape
+    block = summary.shape[0]
     vm = pl.BlockSpec(memory_space=pltpu.VMEM)
     sends = 3 + 3 + 4 + 3 + 3 + 2
     near, every = pl.pallas_call(
@@ -211,31 +231,72 @@
             jax.ShapeDtypeStruct((3, 3, rows, width), BF16),
             jax.ShapeDtypeStruct((2, 4, 4, 2, block, width), BF16),
         ),
-        in_specs=[vm] * 2,
-        out_specs=(vm,) * 2,
+        in_specs=[vm] * 3,
+        out_specs=(pl.BlockSpec(memory_space=pl.ANY),) * 2,
         scratch_shapes=[
+            pltpu.VMEM((rows, width), BF16),
+            pltpu.VMEM((block, width), BF16),
+            pltpu.SemaphoreType.DMA((2,)),
             pltpu.SemaphoreType.DMA((sends,)),
             pltpu.SemaphoreType.DMA((sends,)),
         ],
         compiler_params=pltpu.CompilerParams(
-            collective_id=0, has_side_effects=True, vmem_limit_bytes=32 * 1024 * 1024
+            collective_id=0, has_side_effects=True, vmem_limit_bytes=60 * 1024 * 1024
         ),
         name="gather",
-    )(hidden, summary_hidden)
+    )(tokens, summary, gain)
     return near.reshape(NEAR, rows, width), every.reshape(-1, width)
 
 
 def exchange_kernel(
-    near, own, sums, w_in, gain, out_own, out_sum, w_out, out_gain,
+    near, own, sums, w_in, gain_in, tokens, summary, gain, cot,
+    grad_tokens, grad_summary, grad_gain, w_out,
+    own_v, mid, tok_v, sum_v, gain_v, cot_v, s_loc, w_loc,
     beside, row_sum, z_slot, x_slot, message,
-    s_relay, s_direct, s_one, s_slots_x, s_two, s_slots_y,
+    s_relay, s_direct, s_one, s_slots_x, s_two, s_slots_y, s_sum,
     w_relay, w_direct, w_one, w_slots_two, w_two, w_slots_three,
-    gain_sum, gain_slots, send_sems, recv_sems,
+    gain_sum, gain_slots, local_sems, send_sems, recv_sems,
 ):
     at = places()
     x, y, z = at
     x_hi = lax.axis_index("tx_1")
-    greet(at)
+    met = greet(at)
+    load = Loader(local_sems)
+    width = w_in.shape[1]
+    wide = width // 2
+    part = w_in.shape[0] // 3
+    size = [part // 4, part // 16, part // 64]
+    s_half = sums.shape[0] // 2
+
+    def rows_of(ref, start, count, q):
+        return ref.at[
+            pl.ds(pl.multiple_of(start, PACK), count), q * wide : (q + 1) * wide
+        ]
+
+    def s_piece(d, h):
+        return sums.at[pl.ds(h * s_half, s_half), d]
+
+    def w_piece(p, q):
+        half = size[0] // 2
+        return lambda d, h: rows_of(w_in, p * part + d * size[0] + h * half, half, q)
+
+    def own_pieces(piece, axis, slots):
+        c = at[axis]
+        right, left = lax.rem(c + 1, 4), lax.rem(c + 3, 4)
+        wanted = ((right, 0), (left, 1), (c, 0), (c, 1))
+        return [load.copy(piece(*wanted[k]), slots.at[k]) for k in range(4)]
+
+    w_ready = {
+        (p, q): own_pieces(w_piece(p, q), p, w_loc.at[p, q]) for q in range(2) for p in range(3)
+    }
+    s_ready = own_pieces(s_piece, 2, s_loc)
+    mid_ready = load.copy(near.at[1], mid)
+    gain_ready = load.copy(gain_in, gain_sum.at[0])
+    rest_ready = [
+        load.copy(own, own_v), load.copy(tokens, tok_v), load.copy(summary, sum_v),
+        load.copy(gain, gain_v), load.copy(cot, cot_v),
+    ]
+    met()
     link = Sender(send_sems, recv_sems)
 
     def halo():
@@ -245,109 +306,127 @@
             down = link.send(near.at[0, j], beside.at[1, j], row_peer(at, -1))
             rows.append((j, up, down))
         yield
+        mid_ready.wait()
         for j, up, down in rows[:2]:
             up.wait_recv()
             down.wait_recv()
-            row_sum[j // 2] = added(near.at[1, j], beside.at[0, j], beside.at[1, j]).astype(BF16)
+            row_sum[j // 2] = added(mid.at[j], beside.at[0, j], beside.at[1, j]).astype(BF16)
         there = {"tx_0": lax.rem(z + (3 + 2 * x_hi), 4)}
         far = link.send(row_sum.at[x_hi], z_slot, there)
+        yield
+        far.wait_recv()
+        message[...] = added(row_sum.at[1 - x_hi], z_slot).astype(BF16)
+        last = link.send(message, x_slot, {"tx_1": 1 - x_hi})
         yield
         _, up, down = rows[2]
         up.wait_recv()
         down.wait_recv()
-        out_own[...] = own[...] + added(beside.at[0, 1], beside.at[1, 1])
-        far.wait_recv()
-        message[...] = added(row_sum.at[1 - x_hi], z_slot).astype(BF16)
-        last = link.send(message, x_slot, {"tx_1": 1 - x_hi})
+        for copy in rest_ready:
+            copy.wait()
+        own_v[...] += added(beside.at[0, 1], beside.at[1, 1])
         yield
         yield
         last.wait_recv()
-        out_own[...] += x_slot[...].astype(F32)
+        hidden_grad = own_v[...] + x_slot[...].astype(F32)
+        scale = row_scale(tok_v[...])
+        back = norm_back(tok_v[...], scale, gain_v[...], hidden_grad)
+        grad_tokens[...] = (cot_v[...].astype(F32) + back).astype(BF16)
 
     def summaries():
-        half = sums.shape[0] // 2
         yield from scatter_ring(
-            link, 2, at, lambda d, h: sums.at[pl.ds(h * half, half), d], s_relay, s_direct, s_one
-        )
-        block = out_sum.shape[0]
+            link, 2, at, s_piece, s_loc, s_ready, s_relay, s_direct, s_one
+        )
+        block = summary.shape[0]
         yield from scatter_direct(
             link, 0, at,
             lambda d: s_one.at[lax.rem(d, 2), :, pl.ds((d // 2) * block, block)],
             s_slots_x, s_two,
         )
-        yield from scatter_direct(link, 1, at, lambda d: s_two.at[d], s_slots_y, out_sum)
-
-    def weights(p):
+        yield from scatter_direct(link, 1, at, lambda d: s_two.at[d], s_slots_y, s_sum)
+        scale = row_scale(sum_v[...])
+        back = norm_back(sum_v[...], scale, gain_v[...], s_sum[...])
+        grad_summary[...] = back.astype(BF16)
+
+    def weights(p, q):
         a, b, c = p, (p + 1) % 3, (p + 2) % 3
-        part = w_in.shape[0] // 3
-        size = [part // 4, part // 16, part // 64]
         first = p * part
-
-        def rows_of(ref, start, count):
-            return ref.at[pl.ds(pl.multiple_of(start, PACK), count)]
-
         yield from scatter_ring(
-            link, a, at,
-            lambda d, h: rows_of(w_in, first + d * size[0] + h * (size[0] // 2), size[0] // 2),
-            w_relay.at[p], w_direct.at[p], w_one.at[p],
+            link, a, at, w_piece(p, q), w_loc.at[p, q], w_ready[p, q],
+            w_relay.at[p, q], w_direct.at[p, q], w_one.at[p, q],
         )
         yield from scatter_direct(
             link, b, at,
-            lambda d: w_one.at[p, d // 2, pl.ds(lax.rem(d, 2) * size[1], size[1])],
-            w_slots_two.at[p], w_two.at[p],
+            lambda d: w_one.at[p, q, d // 2, pl.ds(lax.rem(d, 2) * size[1], size[1])],
+            w_slots_two.at[p, q], w_two.at[p, q],
         )
         base = first + at[a] * size[0]
         inner = base + at[b] * size[1]
         yield from scatter_direct(
             link, c, at,
-            lambda d: rows_of(w_two.at[p], d * size[2], size[2]),
-            w_slots_three.at[p],
-            rows_of(w_out, inner + at[c] * size[2], size[2]),
+            lambda d: w_two.at[p, q, pl.ds(pl.multiple_of(d * size[2], PACK), size[2])],
+            w_slots_three.at[p, q],
+            rows_of(w_out, inner + at[c] * size[2], size[2], q),
         )
         yield from gather_direct(
-            link, c, at, lambda d: rows_of(w_out, inner + d * size[2], size[2])
+            link, c, at, lambda d: rows_of(w_out, inner + d * size[2], size[2], q)
         )
         yield from gather_direct(
-            link, b, at, lambda d: rows_of(w_out, base + d * size[1], size[1])
+            link, b, at, lambda d: rows_of(w_out, base + d * size[1], size[1], q)
         )
         yield from gather_ring(
             link, a, at,
-            lambda d: rows_of(w_out, first + d * size[0], size[0]),
+            lambda d: rows_of(w_out, first + d * size[0], size[0], q),
             lambda d, h: rows_of(
-                w_out, first + d * size[0] + h * (size[0] // 2), size[0] // 2
+                w_out, first + d * size[0] + h * (size[0] // 2), size[0] // 2, q
             ),
         )
 
     def gains():
-        gain_sum[0] = gain[...]
+        gain_ready.wait()
         for k in range(3):
             yield from scatter_direct(
-                link, k, at, lambda d, k=k: gain_sum.at[k], gain_slots.at[k],
-                gain_sum.at[k + 1] if k < 2 else out_gain,
+                link, k, at, lambda d, k=k: gain_sum.at[k], gain_slots.at[k], gain_sum.at[k + 1]
             )
-
-    take_turns([halo(), summaries(), weights(0), weights(1), weights(2), gains()])
+        total = jnp.sum(gain_sum[3], axis=0, keepdims=True)
+        grad_gain[...] = total / gain_v[...]
+
+    first_half = [weights(p, 0) for p in range(3)]
+    second_half = [weights(p, 1) for p in range(3)]
+    take_turns([*first_half, halo(), *second_half, summaries(), gains()])
     link.drain()
 
 
-def exchange(near_grad, own_grad, sum_grad, w_part, gain_part, block):
+def exchange(
+    near_grad, own_grad, sum_grad, w_part, gain_part, tokens, summary, norm_gain, cot
+):
     rows, width = own_grad.shape
+    block = summary.shape[0]
     vm = pl.BlockSpec(memory_space=pltpu.VMEM)
     total = w_part.shape[0] * width
     part = total // 3
-    sends = 6 + 2 + 6 + 3 + 3 + 3 * (6 + 3 + 3 + 3 + 3 + 4) + 9
+    wide = width // 2
+    sends = 6 + 2 + 6 + 3 + 3 + 6 * (6 + 3 + 3 + 3 + 3 + 4) + 9
+    loads = 24 + 4 + 2 + 5
     sums = sum_grad.reshape(8, 4, 2 * block, width)
-    own, sum_own, w_all, gain = pl.pallas_call(
+    grad_tokens, grad_summary, gain, w_all = pl.pallas_call(
         exchange_kernel,
         out_shape=(
-            jax.ShapeDtypeStruct((rows, width), F32),
-            jax.ShapeDtypeStruct((block, width), F32),
+            jax.ShapeDtypeStruct((rows, width), BF16),
+            jax.ShapeDtypeStruct((block, width), BF16),
+            jax.ShapeDtypeStruct((1, width), F32),
             jax.ShapeDtypeStruct((total, width), BF16),
-            jax.ShapeDtypeStruct((8, width), F32),
         ),
-        in_specs=[vm] * 5,
+        in_specs=[pl.BlockSpec(memory_space=pl.ANY)] * 9,
         out_specs=(vm,) * 4,
         scratch_shapes=[
+            pltpu.VMEM((rows, width), F32),
+            pltpu.VMEM((3, rows, width), BF16),
+            pltpu.VMEM((rows, width), BF16),
+            pltpu.VMEM((block, width), BF16),
+            pltpu.VMEM((1, width), F32),
+            pltpu.VMEM((rows, width), BF16),
+            pltpu.VMEM((4, 4, 2 * block, width), BF16),
+            pltpu.VMEM((3, 2, 4, part // 8, wide), BF16),
             pltpu.VMEM((2, 3, rows, width), BF16),
             pltpu.VMEM((2, rows, width), BF16),
             pltpu.VMEM((rows, width), BF16),
@@ -359,31 +438,38 @@
             pltpu.VMEM((3, 4, block, width), BF16),
             pltpu.VMEM((4, block, width), BF16),
             pltpu.VMEM((3, block, width), BF16),
-            pltpu.VMEM((3, 2, 2, part // 8, width), BF16),
-            pltpu.VMEM((3, 2, 2, part // 8, width), BF16),
-            pltpu.VMEM((3, 2, part // 8, width), BF16),
-            pltpu.VMEM((3, 3, part // 16, width), BF16),
-            pltpu.VMEM((3, part // 16, width), BF16),
-            pltpu.VMEM((3, 3, part // 64, width), BF16),
-            pltpu.VMEM((3, 8, width), F32),
+            pltpu.VMEM((block, width), F32),
+            pltpu.VMEM((3, 2, 2, 2, part // 8, wide), BF16),
+            pltpu.VMEM((3, 2, 2, 2, part // 8, wide), BF16),
+            pltpu.VMEM((3, 2, 2, part // 8, wide), BF16),
+            pltpu.VMEM((3, 2, 3, part // 16, wide), BF16),
+            pltpu.VMEM((3, 2, part // 16, wide), BF16),
+            pltpu.VMEM((3, 2, 3, part // 64, wide), BF16),
+            pltpu.VMEM((4, 8, width), F32),
             pltpu.VMEM((3, 3, 8, width), F32),
+            pltpu.SemaphoreType.DMA((loads,)),
             pltpu.SemaphoreType.DMA((sends,)),
             pltpu.SemaphoreType.DMA((sends,)),
         ],
         compiler_params=pltpu.CompilerParams(
-            collective_id=1, has_side_effects=True, vmem_limit_bytes=48 * 1024 * 1024
+            collective_id=1, has_side_effects=True, vmem_limit_bytes=60 * 1024 * 1024
         ),
         name="exchange",
     )(
-        near_grad.reshape(3, 3, rows, width), own_grad, sums, w_part.reshape(total, width), gain_part
+        near_grad.reshape(3, 3, rows, width), own_grad, sums, w_part.reshape(total, width),
+        gain_part, tokens, summary, norm_gain, cot,
     )
-    return own, sum_own, w_all.reshape(w_part.shape), jnp.sum(gain, axis=0)
+    return grad_tokens, grad_summary, gain, w_all.reshape(w_part.shape)
+
+
+def row_scale(rows):
+    values = rows.astype(F32)
+    return lax.rsqrt(jnp.mean(values * values, axis=-1, keepdims=True) + epsilon)
 
 
 def normalize(rows, gain):
-    values = rows.astype(F32)
-    scale = lax.rsqrt(jnp.mean(values * values, axis=-1, keepdims=True) + epsilon)
-    return ((values * scale * gain).astype(BF16), scale)
+    scale = row_scale(rows)
+    return ((rows.astype(F32) * scale * gain).astype(BF16), scale)
 
 
 def norm_back(rows, scale, gain, grad_norm):
@@ -397,8 +483,9 @@
 
 
 def layer_kernel(
-    meta, near, summ, w, tok, cot,
-    updated, near_grad, own_grad, sum_grad, w_part, gain_part,
+    counts, pattern, blocks, near, summ, w_in, tok, cot,
+    updated, near_out, own_out, sum_out, w_out, gain_part,
+    w, own_v, near_grad, own_grad, sum_grad, w_part, pack_sems, local_sems,
     xp, kp, vp, dkt, dvt, scores, probs, bias, qs, gs, qst, gst, acc, m_ref, l_ref, d_ref,
     q_all, g_all, o_all, dq_all,
 ):
@@ -413,16 +500,36 @@
     zk = scores.at[:, 0:width]
     zv = scores.at[:, width : 2 * width]
 
+    load = Loader(local_sems)
+    own_ready = load.copy(near.at[NEAR // 2], own_v)
+    w_ready = [load.copy(w_in.at[k], w.at[k]) for k in (0, 3, 1, 2)]
+
+    grid_row = 4 * lax.axis_index("ty_0") + lax.axis_index("ty_1")
+    grid_col = 2 * lax.axis_index("tx_0") + lax.axis_index("tx_1")
+    meta = []
+    for t in range(NEAR):
+        r, c = grid_row + (t // 3 - 1), grid_col + (t % 3 - 1)
+        inside = (r >= 0) & (r < 8) & (c >= 0) & (c < 8)
+        n = counts[jnp.clip(r, 0, 7), jnp.clip(c, 0, 7)]
+        meta.append(jnp.where(inside & (pattern[grid_row, grid_col, t] == 1), n, 0))
+    for b in range(n_blocks):
+        meta.append(jnp.where(blocks[0, 0, b] == 1, 1, 0))
+    meta.append(counts[grid_row, grid_col])
+
+    def packed(k, src, at, size):
+        return pltpu.make_async_copy(
+            src.at[pl.ds(0, size)], xp.at[pl.ds(pl.multiple_of(at, PACK), size)], pack_sems.at[k]
+        )
+
+    packs = []
     block_at = []
     total = jnp.int32(0)
     for b in range(n_blocks):
         block_at.append(total)
         flag = meta[NEAR + b]
 
-        @pl.when(flag == 1)
-        def _(b=b, total=total):
-            xp[pl.ds(pl.multiple_of(total, SBLK), SBLK), :] = summ[b * SBLK : (b + 1) * SBLK, :]
-
+        src = summ.at[pl.ds(b * SBLK, SBLK)]
+        packs.append((flag == 1, packed(NEAR + b, src, total, SBLK)))
         total = total + SBLK * flag
     summ_end = total
     tile_at = []
@@ -430,11 +537,11 @@
         tile_at.append(total)
         n = meta[t]
 
-        @pl.when(n > 0)
-        def _(t=t, total=total):
-            xp[pl.ds(pl.multiple_of(total, PACK), rows), :] = near[t]
-
-        total = total + ((n + (PACK - 1)) // PACK) * PACK
+        size = pl.multiple_of(((n + (PACK - 1)) // PACK) * PACK, PACK)
+        packs.append((n > 0, packed(t, near.at[t], total, size)))
+        total = total + size
+    for live, copy in packs:
+        pl.when(live)(copy.start)
     xp[pl.ds(pl.multiple_of(total, PACK), CHUNK), :] = jnp.zeros((CHUNK, width), BF16)
     chunks = (total + (CHUNK - 1)) // CHUNK
 
@@ -444,11 +551,19 @@
         live = live | ((place >= tile_at[t]) & (place < tile_at[t] + meta[t]))
     bias[...] = jnp.where(live, 0.0, -1e30)
 
-    own = near[NEAR // 2]
+    own_ready.wait()
+    for copy in w_ready[:2]:
+        copy.wait()
+    own = own_v[...]
     valid = lax.broadcasted_iota(jnp.int32, (rows, width), 0) < meta[NEAR + n_blocks]
     masked = jnp.where(valid, cot[...].astype(F32), 0.0).astype(BF16)
     q_all[...] = (dot(own, w[0], 1, 0).astype(BF16).astype(F32) * factor).astype(BF16)
     g_all[...] = dot(masked, w[3], 1, 1).astype(BF16)
+
+    for copy in w_ready[2:]:
+        copy.wait()
+    for live, copy in packs:
+        pl.when(live)(copy.wait)
 
     def project(c, carry):
         at = pl.ds(pl.multiple_of(c * CHUNK, CHUNK), CHUNK)
@@ -532,6 +647,12 @@
             here = slice(i * rows, (i + 1) * rows)
             picked = jnp.where(lane_head == i, dq[here], picked)
         dq_all[:, cols] = picked.astype(BF16)
+
+    w_part[0] = dot(own, dq_all[...], 0, 0).astype(BF16)
+    w_part[3] = dot(o_all[...], masked, 0, 0).astype(BF16)
+    sent = [load.copy(w_part.at[k], w_out.at[k]) for k in (0, 3)]
+    mixed = dot(o_all[...], w[3], 1, 0)
+    updated[...] = (tok[...].astype(F32) + jnp.where(valid, mixed, 0.0)).astype(BF16)
 
     zk[...] = jnp.zeros(zk.shape, F32)
     zv[...] = jnp.zeros(zv.shape, F32)
@@ -557,10 +678,10 @@
 
     lax.fori_loop(0, chunks, finish, 0)
 
-    w_part[0] = dot(own, dq_all[...], 0, 0).astype(BF16)
     w_part[1] = zk[...].astype(BF16).T
+    sent.append(load.copy(w_part.at[1], w_out.at[1]))
     w_part[2] = zv[...].astype(BF16).T
-    w_part[3] = dot(o_all[...], masked, 0, 0).astype(BF16)
+    sent.append(load.copy(w_part.at[2], w_out.at[2]))
 
     row_at = lax.broadcasted_iota(jnp.int32, (rows, width), 0)
     for t in range(NEAR):
@@ -568,23 +689,27 @@
         y = jnp.where(row_at < meta[t], y, 0.0)
         if t == NEAR // 2:
             own_grad[...] = y + own_part
-            near_grad[t] = jnp.zeros((rows, width), BF16)
+            sent.append(load.copy(own_grad, own_out))
         else:
             near_grad[t] = y.astype(BF16)
+            sent.append(load.copy(near_grad.at[t], near_out.at[t]))
     for b in range(n_blocks):
         y = yp[pl.ds(pl.multiple_of(block_at[b], SBLK), SBLK), :].astype(F32)
         keep = jnp.zeros((SBLK, width), jnp.int32) + meta[NEAR + b]
         sum_grad[b * SBLK : (b + 1) * SBLK, :] = jnp.where(keep == 1, y, 0.0).astype(BF16)
-
-    mixed = dot(o_all[...], w[3], 1, 0)
-    updated[...] = (tok[...].astype(F32) + jnp.where(valid, mixed, 0.0)).astype(BF16)
-
-
-def layer(meta, near, summ, w, tok, cot):
+    sent.append(load.copy(sum_grad, sum_out))
+    for copy in sent:
+        copy.wait()
+
+
+def layer(counts, pattern, blocks, near, summ, w, tok, cot):
     rows, width = tok.shape
     most = (NEAR * rows + summ.shape[0] + CHUNK - 1) // CHUNK * CHUNK
     stack = QUAD * rows
     vm = pl.BlockSpec(memory_space=pltpu.VMEM)
+    sm = pl.BlockSpec(memory_space=pltpu.SMEM)
+    far = pl.BlockSpec(memory_space=pl.ANY)
+    n_blocks = summ.shape[0] // SBLK
     return pl.pallas_call(
         layer_kernel,
         out_shape=(
@@ -595,9 +720,17 @@
             jax.ShapeDtypeStruct((4, width, width), BF16),
             jax.ShapeDtypeStruct((8, width), F32),
         ),
-        in_specs=[pl.BlockSpec(memory_space=pltpu.SMEM)] + [vm] * 5,
-        out_specs=(vm,) * 6,
+        in_specs=[sm] * 3 + [far] * 3 + [vm] * 2,
+        out_specs=(vm, far, far, far, far, vm),
         scratch_shapes=[
+            pltpu.VMEM((4, width, width), BF16),
+            pltpu.VMEM((rows, width), BF16),
+            pltpu.VMEM((NEAR, rows, width), BF16),
+            pltpu.VMEM((rows, width), F32),
+            pltpu.VMEM(summ.shape, BF16),
+            pltpu.VMEM((4, width, width), BF16),
+            pltpu.SemaphoreType.DMA((NEAR + n_blocks,)),
+            pltpu.SemaphoreType.DMA((5 + 4 + NEAR + 2,)),
             pltpu.VMEM((most + CHUNK, width), BF16),
             pltpu.VMEM((most + CHUNK, width), BF16),
             pltpu.VMEM((most, width), BF16),
@@ -621,49 +754,29 @@
         ],
         compiler_params=pltpu.CompilerParams(vmem_limit_bytes=63 * 1024 * 1024),
         name="layer",
-    )(meta, near, summ, w, tok, cot)
+    )(counts, pattern, blocks, near, summ, w, tok, cot)
 
 
 def local(
     tokens, summary, counts, tile_pattern, summary_pattern, norm_gain, projections, cotangent
 ):
     rows, width = tokens.shape[2:]
-    zero = jnp.zeros((), jnp.int32)
-    grid_row = lax.axis_index(TY)
-    grid_col = lax.axis_index(TX)
     token_rows = tokens[0, 0]
     grads_in = cotangent[0, 0]
-    hidden, row_scale = normalize(token_rows, norm_gain)
-    summary_hidden, summary_scale = normalize(summary, norm_gain)
-    near, every = gather(hidden, summary_hidden)
-    count_pad = jnp.pad(counts, 1)
-    near_counts = lax.dynamic_slice(count_pad, (grid_row, grid_col), (3, 3)).reshape(NEAR)
-    flags = lax.dynamic_slice(tile_pattern, (grid_row, grid_col, zero), (1, 1, NEAR)).reshape(NEAR)
-    meta = jnp.concatenate(
-        [
-            jnp.where(flags == 1, near_counts, 0),
-            (summary_pattern[0, 0] == 1).astype(jnp.int32),
-            near_counts[NEAR // 2 : NEAR // 2 + 1],
-        ]
+    gain = norm_gain.reshape(1, width)
+    near, every = gather(token_rows, summary, gain)
+    updated, near_grad, own_grad, sum_grad, w_part, gain_part = layer(
+        counts, tile_pattern, summary_pattern, near, every, projections, token_rows, grads_in
     )
-    updated, near_grad, own_grad, sum_grad, w_part, gain_part = layer(
-        meta, near, every, projections, token_rows, grads_in
+    grad_tokens, grad_summary, grad_gain, grad_proj = exchange(
+        near_grad, own_grad, sum_grad, w_part, gain_part, token_rows, summary, gain, grads_in
     )
-    hidden_grad, summary_hidden_grad, grad_proj, grad_gain = exchange(
-        near_grad, own_grad, sum_grad, w_part, gain_part, summary.shape[0]
-    )
-    grad_proj = grad_proj.astype(F32)
-    grad_gain = grad_gain / norm_gain
-    grad_tokens = (
-        grads_in.astype(F32) + norm_back(token_rows, row_scale, norm_gain, hidden_grad)
-    ).astype(BF16)
-    grad_summary = norm_back(summary, summary_scale, norm_gain, summary_hidden_grad).astype(BF16)
     return (
         updated.reshape(tokens.shape),
         grad_tokens.reshape(tokens.shape),
         grad_summary,
-        grad_proj,
-        grad_gain,
+        grad_proj.astype(F32),
+        grad_gain.reshape(width),
     )
 
 

time: 213 us -> 192 us (0.901)
  other arithmetic: 15.9 us -> 8.23 us
  local copies, waits for them, and re-layouts: 9.14 us -> 2.6 us
  Pallas kernels: 187 us -> 181 us
    pallas_call x1, Pallas kernels: 45.5 us -> 32 us  [layer(): pl.pallas_call(layer_kernel, out_shape=(jax.ShapeDtypeStruct((rows, width...]
    pallas_call x1, Pallas kernels: 98.3 us -> 105 us  [exchange(): pl.pallas_call(exchange_kernel, out_shape=(jax.ShapeDtypeStruct((rows, wi...]
    unnamed x20 -> x6, local copies, waits for them, and re-layouts: 7.7 us -> 1.33 us
    convert_element_type x5 -> x1, other arithmetic: 10.2 us -> 6.94 us  [local(): grad_proj.astype(F32)]
    reduce_sum x5 -> x0, other arithmetic: 2.25 us -> none  [the longest x2 1.95 us: normalize(): jnp.mean(values * values, axis=-1, keepdims=True) + epsilon]
where the time goes in v3:
time: 192 us
  Pallas kernels  181 us (94%)
  other arithmetic  8.23 us (4%)
  local copies, waits for them, and re-layouts  2.6 us (1%)
    pallas_call x1, Pallas kernels, exchange(): pl.pallas_call(exchange_kernel, out_shape=(jax.ShapeDtypeStruct((rows, wi...  105 us
    pallas_call x1, Pallas kernels, gather(): pl.pallas_call(gather_kernel, out_shape=(jax.ShapeDtypeStruct((3, 3, rows...  44 us
    pallas_call x1, Pallas kernels, layer(): pl.pallas_call(layer_kernel, out_shape=(jax.ShapeDtypeStruct((rows, width...  32 us
    convert_element_type x1, other arithmetic, local(): grad_proj.astype(F32)  6.94 us

profile of v3, /device:TPU:0, one launch (start us, length us, event | category | flops | bytes accessed | tf_op | source)
XLA Modules:
  0.0 192.2 jit_solution(11909545266236562653)
XLA Ops:
  0.6 1.3 reshape.40.gain
  1.9 44.0 %gather.1 = (bf16[3,3,192,768]{3,2,1,0:T(8,128)(2,1)}, bf16[2,4,4,2,16,768]{5,4,3,2,1,0:T(8,128)(2,1)}) custom-call(bf16[192,768]{1,0:T(8,128)(2,1)} %bitcast.13, bf16[16,768]{1,0:T(8,128)(2,1)} %summary.3, f32[1,768]{1,0:T(1,128)} %reshape.40.gain), custom_call_target="tpu_custom_call" | custom-call | tf_op jit(solution)/shard_map/gather/pallas_call | solution.py:228
  45.9 32.0 %layer.1 = (bf16[192,768]{1,0:T(8,128)(2,1)}, bf16[9,192,768]{2,1,0:T(8,128)(2,1)}, f32[192,768]{1,0:T(8,128)}, bf16[1024,768]{1,0:T(8,128)(2,1)}, bf16[4,768,768]{2,1,0:T(8,128)(2,1)}, /*index=5*/f32[8,768]{1,0:T(8,128)}) custom-call(s32[8,8]{1,0:T(8,128)} %counts.1, s32[8,8,9]{2,1,0:T(8,128)} %pattern.1, s32[1,1,8]{2,1,0:T(1,128)} %blocks.1, ...), custom_call_target="tpu_custom_call" | custom-call | tf_op jit(solution)/shard_map/layer/pallas_call | solution.py:713
  77.9 104.7 %exchange.1 = (bf16[192,768]{1,0:T(8,128)(2,1)}, bf16[16,768]{1,0:T(8,128)(2,1)}, f32[1,768]{1,0:T(1,128)}, bf16[3072,768]{1,0:T(8,128)(2,1)}) custom-call(bf16[3,3,192,768]{3,2,1,0:T(8,128)(2,1)} %bitcast.16, f32[192,768]{1,0:T(8,128)} %get-tuple-element.21.own, bf16[8,4,32,768]{3,2,1,0:T(8,128)(2,1)} %bitcast.18, bf16[3072,768]{1,0:T(8,128)(2,1)} %bitcast.12, ...), custom_call_target="tpu_custom_call" | custom-call | tf_op jit(solution)/shard_map/exchange/pallas_call | solution.py:411
  182.6 1.3 reduce
  183.9 0.0 copy-start
  183.9 0.0 copy-start.1
  183.9 6.9 %convert.1 = f32[4,768,768]{2,1,0:T(8,128)} convert(bf16[4,768,768]{2,1,0:T(8,128)(2,1)} %bitcast.11) | non-fusion elementwise | flops 2359296 | bytes 14155776 | tf_op jit(solution)/shard_map/convert_element_type | solution.py:778
  190.9 0.0 copy-done
  190.9 0.7 copy.15
  191.6 0.0 copy-done.1
  191.6 0.6 copy.16
Async XLA Ops:
  183.9 6.9 %copy-start = (bf16[192,768]{1,0:T(8,128)(2,1)S(1)}, bf16[192,768]{1,0:T(8,128)(2,1)}, u32[]{:S(2)}) copy-start(bf16[192,768]{1,0:T(8,128)(2,1)} %get-tuple-element.25) | copy-start | bytes 884740
  183.9 7.7 %copy-start.1 = (bf16[16,768]{1,0:T(8,128)(2,1)S(1)}, bf16[16,768]{1,0:T(8,128)(2,1)}, u32[]{:S(2)}) copy-start(bf16[16,768]{1,0:T(8,128)(2,1)} %get-tuple-element.36) | copy-start | bytes 73732
